TPU v7x, 32 devices: a whole 2x2x4 slice. The times are simulated.
32 devices in a mesh: group: 2 (over x), date: 16 (over z, y, core).
Axes of the slice: x: 2, y: 2, z: 4, core: 2. Of those that a mesh axis runs over, the one named last changes fastest.
Arguments:
- slc_stack: bfloat16 [16, 2, 32, 16384], P('date', None, 'group'), parts along dimension 2, may hold values from -30 to 30
- band_taps: bfloat16 [2, 2, 32], replicated, may hold values from -1 to 1
- pair_flags: int32 [16, 4], P('date'), may hold values from 0 to 1, as said below
Outputs:
- iono_phase: float32 [16, 8, 1024], P('date', 'group'), parts along dimension 1
- weight_sum: float32 [16, 8, 1024], P('date', 'group'), parts along dimension 1
There are 2 independent parts, one for each index of `group`. A program takes and returns all parts, laid end to end along the dimension named above; an argument that names none is the same for every part. Nothing has to cross between parts.
Inputs may be any that keep to these rules, and one draw needn't show every extreme that they name: pair_flags[d,0] is 1 for every date but the last; pair_flags[d,k] is 0 where d + k + 1 >= 16.
All inputs are finite; a program needn't handle non-finite values.
Results may differ from a plain program's by a relative error of at most 0.002.
Values may be sent and summed in bfloat16 or wider, within the bound.
No kernel may reach another device: no remote copies, remote signals or barrier semaphores. Data moves between devices by JAX's collectives and lax.ppermute only.
A program may use at most 128 MiB of HBM per device.

v0:
```python
import jax
import jax.numpy as jnp
from jax import lax
from jax.sharding import PartitionSpec as P

TAPS = 32
ML_AZ = 4
ML_RG = 16
SPAN = 4
RADIUS = 8
ITERS = 4


eps_power = 1e-06
floor_weight = 0.1
ridge_weight = 0.05
split_coef = 2.0


def shifted(value, axis, steps):
    count = lax.axis_size(axis)
    first, last = (max(0, -steps), min(count, count - steps))
    return lax.ppermute(value, axis, [(source, source + steps) for source in range(first, last)])


def prefix(part, axis, combine, identity):
    place = lax.axis_index(axis)
    gathered = lax.all_gather(part, axis)
    state = jnp.zeros_like(part) + jnp.asarray(identity, part.dtype)

    def one(lap, state):
        return combine(state, lax.dynamic_index_in_dim(gathered, lap, 0, False))

    return lax.fori_loop(0, place, one, state)


def tap_matrix(band_taps):
    coeffs = band_taps.astype(jnp.float32)
    column = lax.broadcasted_iota(jnp.int32, (TAPS, 256, 128), 2)
    source = lax.broadcasted_iota(jnp.int32, (TAPS, 256, 128), 1)
    lagged = lax.broadcasted_iota(jnp.int32, (TAPS, 256, 128), 0)
    selector = (source - column == lagged).astype(jnp.float32)
    toeplitz = jnp.einsum("bru,uji->brji", coeffs, selector)
    upper_half = jnp.stack([toeplitz[:, 0], toeplitz[:, 1]], axis=1)
    bottom = jnp.stack([-toeplitz[:, 1], toeplitz[:, 0]], axis=1)
    matrix = jnp.stack([upper_half, bottom], axis=0)
    return matrix.transpose(0, 3, 1, 2, 4).reshape(512, 512).astype(jnp.bfloat16)


def split_bands(one_scene, matrix):
    row_count = one_scene.shape[1]
    blocks = one_scene.shape[2] // 128
    left_pad = TAPS // 2
    padded = jnp.pad(one_scene, ((0, 0), (0, 0), (left_pad, 128 - left_pad)))
    pieces = padded.reshape(2, row_count, blocks + 1, 128)
    windows = jnp.concatenate([pieces[:, :, :-1], pieces[:, :, 1:]], axis=3)
    windows = windows.transpose(1, 2, 0, 3).reshape(row_count, blocks, 512)
    filtered = jnp.dot(windows, matrix, preferred_element_type=jnp.float32)
    return filtered.astype(jnp.bfloat16).reshape(row_count, blocks, 2, 2, 128)


def multilook(values):
    row_count = values.shape[0]
    blocks = values.shape[1]
    groups = 128 // ML_RG
    summed = values.reshape(row_count // ML_AZ, ML_AZ, blocks, 2, groups, ML_RG).sum(axis=(1, 5))
    return summed.transpose(2, 0, 1, 3).reshape(2, row_count // ML_AZ, blocks * groups)


def band_power(bands):
    real_part = bands[:, :, :, 0].astype(jnp.float32)
    imag_part = bands[:, :, :, 1].astype(jnp.float32)
    return multilook(real_part * real_part + imag_part * imag_part)


def local(slc_stack, band_taps, pair_flags):
    own_scene = slc_stack[0]
    matrix = tap_matrix(band_taps)
    own_bands = split_bands(own_scene, matrix)
    own_power = band_power(own_bands)
    flags = pair_flags[0].astype(jnp.float32)
    looks_wide = own_power.shape[2]
    row_ids = lax.broadcasted_iota(jnp.int32, (looks_wide, looks_wide), 0)
    col_ids = lax.broadcasted_iota(jnp.int32, (looks_wide, looks_wide), 1)
    box_matrix = (jnp.abs(row_ids - col_ids) <= RADIUS).astype(jnp.float32)
    own_real = own_bands[:, :, :, 0].astype(jnp.float32)
    own_imag = own_bands[:, :, :, 1].astype(jnp.float32)
    smooth_list = []
    phase_list = []
    for offset in range(1, SPAN + 1):
        far_scene = shifted(own_scene, "date", -offset)
        partner = split_bands(far_scene, matrix)
        partner_real = partner[:, :, :, 0].astype(jnp.float32)
        partner_imag = partner[:, :, :, 1].astype(jnp.float32)
        cross_real = multilook(own_real * partner_real + own_imag * partner_imag)
        cross_imag = multilook(own_imag * partner_real - own_real * partner_imag)
        partner_power = band_power(partner)
        coherence = (cross_real * cross_real + cross_imag * cross_imag) / (
            own_power * partner_power + eps_power
        )
        weight = flags[offset - 1] * 0.5 * (coherence[0] + coherence[1])
        normalizer = jnp.sqrt(
            (own_power[0] * partner_power[0] + eps_power)
            * (own_power[1] * partner_power[1] + eps_power)
        )
        cross_term = cross_imag[0] * cross_real[1] - cross_real[0] * cross_imag[1]
        raw_phase = split_coef * cross_term / normalizer
        stacked = jnp.concatenate([weight * raw_phase, weight], axis=0)
        smoothed = jnp.matmul(stacked, box_matrix, precision=lax.Precision.HIGHEST)
        look_rows = weight.shape[0]
        numerator = smoothed[:look_rows]
        denominator = smoothed[look_rows:]
        phase_list.append(numerator / (denominator + floor_weight))
        smooth_list.append(denominator / (2 * RADIUS + 1))
    chain_start = prefix(
        phase_list[0], "date", lambda former, latter: former + latter, jnp.zeros_like(phase_list[0])
    )
    low_weight = []
    low_phase = []
    for offset in range(1, SPAN + 1):
        packed = jnp.stack([smooth_list[offset - 1], phase_list[offset - 1]], axis=0)
        received = shifted(packed, "date", offset)
        low_weight.append(received[0])
        low_phase.append(received[1])
    weight_sum = jnp.zeros_like(chain_start)
    for offset in range(1, SPAN + 1):
        weight_sum = weight_sum + smooth_list[offset - 1] + low_weight[offset - 1]
    diagonal = weight_sum + ridge_weight
    iono_phase = chain_start
    for sweep_index in range(ITERS):
        accumulated = ridge_weight * chain_start
        for offset in range(1, SPAN + 1):
            later_value = shifted(iono_phase, "date", -offset)
            earlier_value = shifted(iono_phase, "date", offset)
            accumulated = accumulated + smooth_list[offset - 1] * (
                later_value - phase_list[offset - 1]
            )
            accumulated = accumulated + low_weight[offset - 1] * (
                earlier_value + low_phase[offset - 1]
            )
        iono_phase = accumulated / diagonal
    return (iono_phase[None], weight_sum[None])


def solution(mesh):
    in_specs = (P("date", None, "group", None), P(), P("date", None))
    out_specs = (P("date", "group", None), P("date", "group", None))
    return jax.shard_map(local, mesh=mesh, in_specs=in_specs, out_specs=out_specs, check_vma=False)
```

profile of v0, /device:TPU:0, one launch (start us, length us, event | category | flops | bytes accessed | tf_op | source)
XLA Modules:
  0.0 305.9 jit_solution(17553632208209028197)
XLA Ops:
  12.2 2.6 convolution_convert_fusion.4
  14.8 2.5 reshape.355
  17.4 4.2 %fusion.85 = (bf16[16,128,2,1,128]{4,3,2,1,0:T(2,128)(2,1)}, bf16[16,128,2,1,128]{4,3,2,1,0:T(2,128)(2,1)}) fusion(bf16[16,128,2,2,128]{4,3,2,1,0:T(2,128)(2,1)S(1)} %reshape.355), kind=kLoop, calls=%fused_computation.173 | loop fusion | bytes 4194304 | tf_op jit(solution)/shard_map/slice | solution.py:87
  21.6 4.7 %copy.54 = bf16[16,128,2,1,128]{1,4,2,0,3:T(8,128)(2,1)S(1)} copy(bf16[16,128,2,1,128]{4,3,2,1,0:T(2,128)(2,1)} %get-tuple-element.62) | data formatting | bytes 2097152
  26.4 3.4 %copy.56 = bf16[16,128,2,1,128]{1,4,2,0,3:T(8,128)(2,1)} copy(bf16[16,128,2,1,128]{4,3,2,1,0:T(2,128)(2,1)S(1)} %copy-done.4) | data formatting | bytes 2097152
  36.8 2.6 convolution_convert_fusion.3
  39.5 2.5 reshape.358
  42.0 4.2 %fusion.86 = (bf16[16,128,2,1,128]{4,3,2,1,0:T(2,128)(2,1)}, bf16[16,128,2,1,128]{4,3,2,1,0:T(2,128)(2,1)}) fusion(bf16[16,128,2,2,128]{4,3,2,1,0:T(2,128)(2,1)S(1)} %reshape.358), kind=kLoop, calls=%fused_computation.174 | loop fusion | bytes 4194304 | tf_op jit(solution)/shard_map/slice | solution.py:94
  50.3 2.7 convolution_convert_fusion.1
  52.9 2.5 reshape.364
  55.5 4.2 %fusion.83 = (bf16[16,128,2,1,128]{4,3,2,1,0:T(2,128)(2,1)}, bf16[16,128,2,1,128]{4,3,2,1,0:T(2,128)(2,1)}) fusion(bf16[16,128,2,2,128]{4,3,2,1,0:T(2,128)(2,1)S(1)} %reshape.364), kind=kLoop, calls=%fused_computation.171 | loop fusion | bytes 4194304 | tf_op jit(solution)/shard_map/slice | solution.py:94
  59.7 14.0 %collective-permute-done.12 = bf16[2,16,16384]{2,1,0:T(8,128)(2,1)} collective-permute-done((bf16[2,16,16384]{2,1,0:T(8,128)(2,1)}, bf16[2,16,16384]{2,1,0:T(8,128)(2,1)}, u32[]{:S(2)}, u32[]{:S(2)}) %collective-permute-start.12) | collective-permute-done | bytes 1048608 | tf_op jit(solution)/shard_map/ppermute | solution.py:23
  77.9 2.7 convolution_convert_fusion
  80.6 5.9 %copy.55 = bf16[16,128,2,1,128]{1,4,2,0,3:T(8,128)(2,1)} copy(bf16[16,128,2,1,128]{4,3,2,1,0:T(2,128)(2,1)} %get-tuple-element.64) | data formatting | bytes 2097152
  86.5 3.4 %copy.57 = bf16[16,128,2,1,128]{1,4,2,0,3:T(8,128)(2,1)} copy(bf16[16,128,2,1,128]{4,3,2,1,0:T(2,128)(2,1)S(1)} %copy-done.2) | data formatting | bytes 2097152
  89.9 5.9 %copy.60 = bf16[16,128,2,1,128]{1,4,2,0,3:T(8,128)(2,1)} copy(bf16[16,128,2,1,128]{4,3,2,1,0:T(2,128)(2,1)} %get-tuple-element.58) | data formatting | bytes 2097152
  95.8 3.4 %copy.61 = bf16[16,128,2,1,128]{1,4,2,0,3:T(8,128)(2,1)} copy(bf16[16,128,2,1,128]{4,3,2,1,0:T(2,128)(2,1)S(1)} %copy-done.3) | data formatting | bytes 2097152
  99.2 2.5 reshape.367
  101.8 4.2 %fusion.84 = (bf16[16,128,2,1,128]{4,3,2,1,0:T(2,128)(2,1)}, bf16[16,128,2,1,128]{4,3,2,1,0:T(2,128)(2,1)}) fusion(bf16[16,128,2,2,128]{4,3,2,1,0:T(2,128)(2,1)S(1)} %reshape.367), kind=kLoop, calls=%fused_computation.172 | loop fusion | bytes 4194304 | tf_op jit(solution)/shard_map/slice | solution.py:94
  106.0 5.9 %copy.62 = bf16[16,128,2,1,128]{1,4,2,0,3:T(8,128)(2,1)} copy(bf16[16,128,2,1,128]{4,3,2,1,0:T(2,128)(2,1)} %get-tuple-element.60) | data formatting | bytes 2097152
  111.9 3.3 %copy.63 = bf16[16,128,2,1,128]{1,4,2,0,3:T(8,128)(2,1)} copy(bf16[16,128,2,1,128]{4,3,2,1,0:T(2,128)(2,1)S(1)} %copy-done.5) | data formatting | bytes 2097152
  119.3 2.6 convolution_convert_fusion.2
  121.9 2.5 reshape.361
  124.5 4.2 %fusion.82 = (bf16[16,128,2,1,128]{4,3,2,1,0:T(2,128)(2,1)}, bf16[16,128,2,1,128]{4,3,2,1,0:T(2,128)(2,1)}) fusion(bf16[16,128,2,2,128]{4,3,2,1,0:T(2,128)(2,1)S(1)} %reshape.361), kind=kLoop, calls=%fused_computation.170 | loop fusion | bytes 4194304 | tf_op jit(solution)/shard_map/slice | solution.py:94
  128.7 5.9 %copy.58 = bf16[16,128,2,1,128]{1,4,2,0,3:T(8,128)(2,1)} copy(bf16[16,128,2,1,128]{4,3,2,1,0:T(2,128)(2,1)} %get-tuple-element.56) | data formatting | bytes 2097152
  134.6 3.3 %copy.59 = bf16[16,128,2,1,128]{1,4,2,0,3:T(8,128)(2,1)} copy(bf16[16,128,2,1,128]{4,3,2,1,0:T(2,128)(2,1)S(1)} %copy-done.6) | data formatting | bytes 2097152
  138.0 11.7 %fusion.10 = (f32[16,128,2,1,128]{1,4,2,0,3:T(8,128)}, f32[16,128,2,1,128]{1,4,2,0,3:T(8,128)}, f32[16,128,2,1,128]{1,4,2,0,3:T(8,128)}, f32[16,128,2,1,128]{1,4...) fusion(bf16[16,128,2,1,128]{1,4,2,0,3:T(8,128)(2,1)} %copy.58, ...), kind=kLoop, calls=%fused_computation.38 | loop fusion | flops 25690112 | bytes 37748736 | tf_op jit(solution)/shard_map/add | solution.py:95
  173.1 17.8 %all-gather.1 = f32[16,4,1024]{2,1,0:T(4,128)S(1)} all-gather(f32[1,4,1024]{2,1,0:T(4,128)S(1)} %bitcast.251), channel_id=2, replica_groups=mesh['group'=2,'date'=16] {'date'}, dimensions={0}, use_global_device_ids=true | all-gather | bytes 278528 | tf_op jit(solution)/shard_map/all_gather | solution.py:28
  192.3 4.7 %collective-permute-start.11 = (f32[4,1024]{1,0:T(4,128)S(1)}, f32[4,1024]{1,0:T(4,128)S(1)}, u32[]{:S(2)}, u32[]{:S(2)}) collective-permute-start(f32[4,1024]{1,0:T(4,128)S(1)} %get-tuple-element.25), channel_id=1, source_target_pairs={{0,3},{1,4},{2,5},{3,6},{4,7},{5,8},{6,9},{7,10},{8,11},{9,12},{10... | collective-permute-start | bytes 49160 | tf_op jit(solution)/shard_map/ppermute | solution.py:23
  198.3 4.5 %collective-permute-start.15 = (f32[4,1024]{1,0:T(4,128)S(1)}, f32[4,1024]{1,0:T(4,128)S(1)}, u32[]{:S(2)}, u32[]{:S(2)}) collective-permute-start(f32[4,1024]{1,0:T(4,128)S(1)} %get-tuple-element.25), channel_id=1, source_target_pairs={{0,4},{1,5},{2,6},{3,7},{4,8},{5,9},{6,10},{7,11},{8,12},{9,13},{1... | collective-permute-start | bytes 49160 | tf_op jit(solution)/shard_map/ppermute | solution.py:23
  202.8 2.8 collective-permute-start.3
  210.7 4.5 %collective-permute-start.7 = (f32[4,1024]{1,0:T(4,128)S(1)}, f32[4,1024]{1,0:T(4,128)S(1)}, u32[]{:S(2)}, u32[]{:S(2)}) collective-permute-start(f32[4,1024]{1,0:T(4,128)S(1)} %get-tuple-element.25), channel_id=1, source_target_pairs={{0,2},{1,3},{2,4},{3,5},{4,6},{5,7},{6,8},{7,9},{8,10},{9,11},{10,... | collective-permute-start | bytes 49160 | tf_op jit(solution)/shard_map/ppermute | solution.py:23
  215.2 2.4 collective-permute-start.14
  217.6 3.1 %collective-permute-start.10 = (f32[2,4,1024]{2,1,0:T(4,128)S(1)}, f32[2,4,1024]{2,1,0:T(4,128)S(1)}, u32[]{:S(2)}, u32[]{:S(2)}) collective-permute-start(f32[2,4,1024]{2,1,0:T(4,128)S(1)} %pad_maximum_fusion.2), channel_id=1, source_target_pairs={{0,3},{1,4},{2,5},{3,6},{4,7},{5,8},{6,9},{7,10},{8,11},{9,12},{10... | collective-permute-start | bytes 98312 | tf_op jit(solution)/shard_map/ppermute | solution.py:23
  220.8 2.5 collective-permute-start.6
  226.1 3.8 %collective-permute-done.9 = f32[4,1024]{1,0:T(4,128)S(1)} collective-permute-done((f32[4,1024]{1,0:T(4,128)S(1)}, f32[4,1024]{1,0:T(4,128)S(1)}, u32[]{:S(2)}, u32[]{:S(2)}) %collective-permute-start.9) | collective-permute-done | bytes 16416 | tf_op jit(solution)/shard_map/ppermute | solution.py:23
  231.2 4.3 %collective-permute-start.17 = (f32[4,1024]{1,0:T(4,128)S(1)}, f32[4,1024]{1,0:T(4,128)S(1)}, u32[]{:S(2)}, u32[]{:S(2)}) collective-permute-start(f32[4,1024]{1,0:T(4,128)S(1)} %get-tuple-element.34), channel_id=1, source_target_pairs={{0,1},{1,2},{2,3},{3,4},{4,5},{5,6},{6,7},{7,8},{8,9},{9,10},{10,1... | collective-permute-start | bytes 49160 | tf_op jit(solution)/shard_map/ppermute | solution.py:23
  236.8 4.5 %collective-permute-start.19 = (f32[4,1024]{1,0:T(4,128)S(1)}, f32[4,1024]{1,0:T(4,128)S(1)}, u32[]{:S(2)}, u32[]{:S(2)}) collective-permute-start(f32[4,1024]{1,0:T(4,128)S(1)} %get-tuple-element.34), channel_id=1, source_target_pairs={{0,2},{1,3},{2,4},{3,5},{4,6},{5,7},{6,8},{7,9},{8,10},{9,11},{10,... | collective-permute-start | bytes 49160 | tf_op jit(solution)/shard_map/ppermute | solution.py:23
  242.7 5.7 %collective-permute-start.21 = (f32[4,1024]{1,0:T(4,128)S(1)}, f32[4,1024]{1,0:T(4,128)S(1)}, u32[]{:S(2)}, u32[]{:S(2)}) collective-permute-start(f32[4,1024]{1,0:T(4,128)S(1)} %get-tuple-element.34), channel_id=1, source_target_pairs={{0,3},{1,4},{2,5},{3,6},{4,7},{5,8},{6,9},{7,10},{8,11},{9,12},{10... | collective-permute-start | bytes 49160 | tf_op jit(solution)/shard_map/ppermute | solution.py:23
  249.7 4.5 %collective-permute-start.23 = (f32[4,1024]{1,0:T(4,128)S(1)}, f32[4,1024]{1,0:T(4,128)S(1)}, u32[]{:S(2)}, u32[]{:S(2)}) collective-permute-start(f32[4,1024]{1,0:T(4,128)S(1)} %get-tuple-element.34), channel_id=1, source_target_pairs={{0,4},{1,5},{2,6},{3,7},{4,8},{5,9},{6,10},{7,11},{8,12},{9,13},{1... | collective-permute-start | bytes 49160 | tf_op jit(solution)/shard_map/ppermute | solution.py:23
  257.1 3.0 collective-permute-start.25
  261.4 4.5 %collective-permute-start.27 = (f32[4,1024]{1,0:T(4,128)S(1)}, f32[4,1024]{1,0:T(4,128)S(1)}, u32[]{:S(2)}, u32[]{:S(2)}) collective-permute-start(f32[4,1024]{1,0:T(4,128)S(1)} %add_divide_fusion.6), channel_id=1, source_target_pairs={{0,2},{1,3},{2,4},{3,5},{4,6},{5,7},{6,8},{7,9},{8,10},{9,11},{10,... | collective-permute-start | bytes 49160 | tf_op jit(solution)/shard_map/ppermute | solution.py:23
  267.3 5.9 %collective-permute-start.29 = (f32[4,1024]{1,0:T(4,128)S(1)}, f32[4,1024]{1,0:T(4,128)S(1)}, u32[]{:S(2)}, u32[]{:S(2)}) collective-permute-start(f32[4,1024]{1,0:T(4,128)S(1)} %add_divide_fusion.6), channel_id=1, source_target_pairs={{0,3},{1,4},{2,5},{3,6},{4,7},{5,8},{6,9},{7,10},{8,11},{9,12},{10... | collective-permute-start | bytes 49160 | tf_op jit(solution)/shard_map/ppermute | solution.py:23
  274.5 4.5 %collective-permute-start.31 = (f32[4,1024]{1,0:T(4,128)S(1)}, f32[4,1024]{1,0:T(4,128)S(1)}, u32[]{:S(2)}, u32[]{:S(2)}) collective-permute-start(f32[4,1024]{1,0:T(4,128)S(1)} %add_divide_fusion.6), channel_id=1, source_target_pairs={{0,4},{1,5},{2,6},{3,7},{4,8},{5,9},{6,10},{7,11},{8,12},{9,13},{1... | collective-permute-start | bytes 49160 | tf_op jit(solution)/shard_map/ppermute | solution.py:23
  281.8 3.0 collective-permute-start.33
  286.2 5.0 %collective-permute-start.35 = (f32[4,1024]{1,0:T(4,128)S(1)}, f32[4,1024]{1,0:T(4,128)S(1)}, u32[]{:S(2)}, u32[]{:S(2)}) collective-permute-start(f32[4,1024]{1,0:T(4,128)S(1)} %add_divide_fusion.5), channel_id=1, source_target_pairs={{0,2},{1,3},{2,4},{3,5},{4,6},{5,7},{6,8},{7,9},{8,10},{9,11},{10,... | collective-permute-start | bytes 49160 | tf_op jit(solution)/shard_map/ppermute | solution.py:23
  292.5 5.4 %collective-permute-start.37 = (f32[4,1024]{1,0:T(4,128)S(1)}, f32[4,1024]{1,0:T(4,128)S(1)}, u32[]{:S(2)}, u32[]{:S(2)}) collective-permute-start(f32[4,1024]{1,0:T(4,128)S(1)} %add_divide_fusion.5), channel_id=1, source_target_pairs={{0,3},{1,4},{2,5},{3,6},{4,7},{5,8},{6,9},{7,10},{8,11},{9,12},{10... | collective-permute-start | bytes 49160 | tf_op jit(solution)/shard_map/ppermute | solution.py:23
  299.2 4.5 %collective-permute-start.39 = (f32[4,1024]{1,0:T(4,128)S(1)}, f32[4,1024]{1,0:T(4,128)S(1)}, u32[]{:S(2)}, u32[]{:S(2)}) collective-permute-start(f32[4,1024]{1,0:T(4,128)S(1)} %add_divide_fusion.5), channel_id=1, source_target_pairs={{0,4},{1,5},{2,6},{3,7},{4,8},{5,9},{6,10},{7,11},{8,12},{9,13},{1... | collective-permute-start | bytes 49160 | tf_op jit(solution)/shard_map/ppermute | solution.py:23
  (177 shorter events, 82.3 us)
Async XLA Ops:
  0.6 5.2 %copy-start = (bf16[2,2,32]{2,1,0:T(2,128)(2,1)S(1)}, bf16[2,2,32]{2,1,0:T(2,128)(2,1)}, u32[]{:S(2)}) copy-start(bf16[2,2,32]{2,1,0:T(2,128)(2,1)} %param.6) | copy-start | bytes 772
  0.6 32.1 %collective-permute-start = (bf16[2,16,16384]{2,1,0:T(8,128)(2,1)}, bf16[2,16,16384]{2,1,0:T(8,128)(2,1)}, u32[]{:S(2)}, u32[]{:S(2)}) collective-permute-start(bf16[2,16,16384]{2,1,0:T(8,128)(2,1)} %bitcast.244), channel_id=1, source_target_pairs={{1,0},{2,1},{3,2},{4,3},{5,4},{6,5},{7,6},{8,7},{9,8},{10,9},{11,1... | collective-permute-start | bytes 3145736 | tf_op jit(solution)/shard_map/ppermute | solution.py:23
  1.9 44.3 %collective-permute-start.8 = (bf16[2,16,16384]{2,1,0:T(8,128)(2,1)}, bf16[2,16,16384]{2,1,0:T(8,128)(2,1)}, u32[]{:S(2)}, u32[]{:S(2)}) collective-permute-start(bf16[2,16,16384]{2,1,0:T(8,128)(2,1)} %bitcast.245), channel_id=1, source_target_pairs={{3,0},{4,1},{5,2},{6,3},{7,4},{8,5},{9,6},{10,7},{11,8},{12,9},{13... | collective-permute-start | bytes 3145736 | tf_op jit(solution)/shard_map/ppermute | solution.py:23
  3.2 70.4 %collective-permute-start.12 = (bf16[2,16,16384]{2,1,0:T(8,128)(2,1)}, bf16[2,16,16384]{2,1,0:T(8,128)(2,1)}, u32[]{:S(2)}, u32[]{:S(2)}) collective-permute-start(bf16[2,16,16384]{2,1,0:T(8,128)(2,1)} %bitcast.246), channel_id=1, source_target_pairs={{4,0},{5,1},{6,2},{7,3},{8,4},{9,5},{10,6},{11,7},{12,8},{13,9},{1... | collective-permute-start | bytes 3145736 | tf_op jit(solution)/shard_map/ppermute | solution.py:23
  4.5 110.7 %collective-permute-start.4 = (bf16[2,16,16384]{2,1,0:T(8,128)(2,1)}, bf16[2,16,16384]{2,1,0:T(8,128)(2,1)}, u32[]{:S(2)}, u32[]{:S(2)}) collective-permute-start(bf16[2,16,16384]{2,1,0:T(8,128)(2,1)} %bitcast.247), channel_id=1, source_target_pairs={{2,0},{3,1},{4,2},{5,3},{6,4},{7,5},{8,6},{9,7},{10,8},{11,9},{12,... | collective-permute-start | bytes 3145736 | tf_op jit(solution)/shard_map/ppermute | solution.py:23
  21.6 4.8 %copy-start.4 = (bf16[16,128,2,1,128]{4,3,2,1,0:T(2,128)(2,1)S(1)}, bf16[16,128,2,1,128]{4,3,2,1,0:T(2,128)(2,1)}, u32[]{:S(2)}) copy-start(bf16[16,128,2,1,128]{4,3,2,1,0:T(2,128)(2,1)} %get-tuple-element.61) | copy-start | bytes 3145732
  80.6 5.9 %copy-start.2 = (bf16[16,128,2,1,128]{4,3,2,1,0:T(2,128)(2,1)S(1)}, bf16[16,128,2,1,128]{4,3,2,1,0:T(2,128)(2,1)}, u32[]{:S(2)}) copy-start(bf16[16,128,2,1,128]{4,3,2,1,0:T(2,128)(2,1)} %get-tuple-element.63) | copy-start | bytes 3145732
  89.9 5.9 %copy-start.3 = (bf16[16,128,2,1,128]{4,3,2,1,0:T(2,128)(2,1)S(1)}, bf16[16,128,2,1,128]{4,3,2,1,0:T(2,128)(2,1)}, u32[]{:S(2)}) copy-start(bf16[16,128,2,1,128]{4,3,2,1,0:T(2,128)(2,1)} %get-tuple-element.57) | copy-start | bytes 3145732
  106.0 5.9 %copy-start.5 = (bf16[16,128,2,1,128]{4,3,2,1,0:T(2,128)(2,1)S(1)}, bf16[16,128,2,1,128]{4,3,2,1,0:T(2,128)(2,1)}, u32[]{:S(2)}) copy-start(bf16[16,128,2,1,128]{4,3,2,1,0:T(2,128)(2,1)} %get-tuple-element.59) | copy-start | bytes 3145732
  128.7 5.9 %copy-start.6 = (bf16[16,128,2,1,128]{4,3,2,1,0:T(2,128)(2,1)S(1)}, bf16[16,128,2,1,128]{4,3,2,1,0:T(2,128)(2,1)}, u32[]{:S(2)}) copy-start(bf16[16,128,2,1,128]{4,3,2,1,0:T(2,128)(2,1)} %get-tuple-element.55) | copy-start | bytes 3145732
  191.0 18.3 %collective-permute-start.1 = (f32[4,1024]{1,0:T(4,128)S(1)}, f32[4,1024]{1,0:T(4,128)S(1)}, u32[]{:S(2)}, u32[]{:S(2)}) collective-permute-start(f32[4,1024]{1,0:T(4,128)S(1)} %get-tuple-element.25), channel_id=1, source_target_pairs={{1,0},{2,1},{3,2},{4,3},{5,4},{6,5},{7,6},{8,7},{9,8},{10,9},{11,1... | collective-permute-start | bytes 49160 | tf_op jit(solution)/shard_map/ppermute | solution.py:23
  192.3 18.4 %collective-permute-start.11 = (f32[4,1024]{1,0:T(4,128)S(1)}, f32[4,1024]{1,0:T(4,128)S(1)}, u32[]{:S(2)}, u32[]{:S(2)}) collective-permute-start(f32[4,1024]{1,0:T(4,128)S(1)} %get-tuple-element.25), channel_id=1, source_target_pairs={{0,3},{1,4},{2,5},{3,6},{4,7},{5,8},{6,9},{7,10},{8,11},{9,12},{10... | collective-permute-start | bytes 49160 | tf_op jit(solution)/shard_map/ppermute | solution.py:23
  197.0 18.2 %collective-permute-start.13 = (f32[4,1024]{1,0:T(4,128)S(1)}, f32[4,1024]{1,0:T(4,128)S(1)}, u32[]{:S(2)}, u32[]{:S(2)}) collective-permute-start(f32[4,1024]{1,0:T(4,128)S(1)} %get-tuple-element.25), channel_id=1, source_target_pairs={{4,0},{5,1},{6,2},{7,3},{8,4},{9,5},{10,6},{11,7},{12,8},{13,9},{1... | collective-permute-start | bytes 49160 | tf_op jit(solution)/shard_map/ppermute | solution.py:23
  198.3 19.3 %collective-permute-start.15 = (f32[4,1024]{1,0:T(4,128)S(1)}, f32[4,1024]{1,0:T(4,128)S(1)}, u32[]{:S(2)}, u32[]{:S(2)}) collective-permute-start(f32[4,1024]{1,0:T(4,128)S(1)} %get-tuple-element.25), channel_id=1, source_target_pairs={{0,4},{1,5},{2,6},{3,7},{4,8},{5,9},{6,10},{7,11},{8,12},{9,13},{1... | collective-permute-start | bytes 49160 | tf_op jit(solution)/shard_map/ppermute | solution.py:23
  202.8 17.9 %collective-permute-start.3 = (f32[4,1024]{1,0:T(4,128)S(1)}, f32[4,1024]{1,0:T(4,128)S(1)}, u32[]{:S(2)}, u32[]{:S(2)}) collective-permute-start(f32[4,1024]{1,0:T(4,128)S(1)} %get-tuple-element.25), channel_id=1, source_target_pairs={{0,1},{1,2},{2,3},{3,4},{4,5},{5,6},{6,7},{7,8},{8,9},{9,10},{10,1... | collective-permute-start | bytes 49160 | tf_op jit(solution)/shard_map/ppermute | solution.py:23
  208.7 97.2 %copy-start.1 = (bf16[2,2,32]{2,1,0:T(2,128)(2,1)S(1)}, bf16[2,2,32]{2,1,0:T(2,128)(2,1)}, u32[]{:S(2)}) copy-start(bf16[2,2,32]{2,1,0:T(2,128)(2,1)} %param.6) | copy-start | bytes 772
  209.3 14.0 %collective-permute-start.5 = (f32[4,1024]{1,0:T(4,128)S(1)}, f32[4,1024]{1,0:T(4,128)S(1)}, u32[]{:S(2)}, u32[]{:S(2)}) collective-permute-start(f32[4,1024]{1,0:T(4,128)S(1)} %get-tuple-element.25), channel_id=1, source_target_pairs={{2,0},{3,1},{4,2},{5,3},{6,4},{7,5},{8,6},{9,7},{10,8},{11,9},{12,... | collective-permute-start | bytes 49160 | tf_op jit(solution)/shard_map/ppermute | solution.py:23
  210.7 14.1 %collective-permute-start.7 = (f32[4,1024]{1,0:T(4,128)S(1)}, f32[4,1024]{1,0:T(4,128)S(1)}, u32[]{:S(2)}, u32[]{:S(2)}) collective-permute-start(f32[4,1024]{1,0:T(4,128)S(1)} %get-tuple-element.25), channel_id=1, source_target_pairs={{0,2},{1,3},{2,4},{3,5},{4,6},{5,7},{6,8},{7,9},{8,10},{9,11},{10,... | collective-permute-start | bytes 49160 | tf_op jit(solution)/shard_map/ppermute | solution.py:23
  215.2 14.6 %collective-permute-start.14 = (f32[2,4,1024]{2,1,0:T(4,128)S(1)}, f32[2,4,1024]{2,1,0:T(4,128)S(1)}, u32[]{:S(2)}, u32[]{:S(2)}) collective-permute-start(f32[2,4,1024]{2,1,0:T(4,128)S(1)} %pad_maximum_fusion.3), channel_id=1, source_target_pairs={{0,4},{1,5},{2,6},{3,7},{4,8},{5,9},{6,10},{7,11},{8,12},{9,13},{1... | collective-permute-start | bytes 98312 | tf_op jit(solution)/shard_map/ppermute | solution.py:23
  217.6 12.2 %collective-permute-start.10 = (f32[2,4,1024]{2,1,0:T(4,128)S(1)}, f32[2,4,1024]{2,1,0:T(4,128)S(1)}, u32[]{:S(2)}, u32[]{:S(2)}) collective-permute-start(f32[2,4,1024]{2,1,0:T(4,128)S(1)} %pad_maximum_fusion.2), channel_id=1, source_target_pairs={{0,3},{1,4},{2,5},{3,6},{4,7},{5,8},{6,9},{7,10},{8,11},{9,12},{10... | collective-permute-start | bytes 98312 | tf_op jit(solution)/shard_map/ppermute | solution.py:23
  220.8 9.0 %collective-permute-start.6 = (f32[2,4,1024]{2,1,0:T(4,128)S(1)}, f32[2,4,1024]{2,1,0:T(4,128)S(1)}, u32[]{:S(2)}, u32[]{:S(2)}) collective-permute-start(f32[2,4,1024]{2,1,0:T(4,128)S(1)} %pad_maximum_fusion.1), channel_id=1, source_target_pairs={{0,2},{1,3},{2,4},{3,5},{4,6},{5,7},{6,8},{7,9},{8,10},{9,11},{10,... | collective-permute-start | bytes 98312 | tf_op jit(solution)/shard_map/ppermute | solution.py:23
  223.3 6.6 %collective-permute-start.2 = (f32[2,4,1024]{2,1,0:T(4,128)S(1)}, f32[2,4,1024]{2,1,0:T(4,128)S(1)}, u32[]{:S(2)}, u32[]{:S(2)}) collective-permute-start(f32[2,4,1024]{2,1,0:T(4,128)S(1)} %pad_maximum_fusion), channel_id=1, source_target_pairs={{0,1},{1,2},{2,3},{3,4},{4,5},{5,6},{6,7},{7,8},{8,9},{9,10},{10,1... | collective-permute-start | bytes 98312 | tf_op jit(solution)/shard_map/ppermute | solution.py:23
  224.8 5.1 %collective-permute-start.9 = (f32[4,1024]{1,0:T(4,128)S(1)}, f32[4,1024]{1,0:T(4,128)S(1)}, u32[]{:S(2)}, u32[]{:S(2)}) collective-permute-start(f32[4,1024]{1,0:T(4,128)S(1)} %get-tuple-element.25), channel_id=1, source_target_pairs={{3,0},{4,1},{5,2},{6,3},{7,4},{8,5},{9,6},{10,7},{11,8},{12,9},{13... | collective-permute-start | bytes 49160 | tf_op jit(solution)/shard_map/ppermute | solution.py:23
  229.9 75.9 %copy-start.13 = (f32[4,1024]{1,0:T(4,128)}, f32[4,1024]{1,0:T(4,128)S(1)}, u32[]{:S(2)}) copy-start(f32[4,1024]{1,0:T(4,128)S(1)} %get-tuple-element.35) | copy-start | bytes 49156
  229.9 12.7 %collective-permute-start.16 = (f32[4,1024]{1,0:T(4,128)S(1)}, f32[4,1024]{1,0:T(4,128)S(1)}, u32[]{:S(2)}, u32[]{:S(2)}) collective-permute-start(f32[4,1024]{1,0:T(4,128)S(1)} %get-tuple-element.34), channel_id=1, source_target_pairs={{1,0},{2,1},{3,2},{4,3},{5,4},{6,5},{7,6},{8,7},{9,8},{10,9},{11,1... | collective-permute-start | bytes 49160 | tf_op jit(solution)/shard_map/ppermute | solution.py:23
  231.2 17.2 %collective-permute-start.17 = (f32[4,1024]{1,0:T(4,128)S(1)}, f32[4,1024]{1,0:T(4,128)S(1)}, u32[]{:S(2)}, u32[]{:S(2)}) collective-permute-start(f32[4,1024]{1,0:T(4,128)S(1)} %get-tuple-element.34), channel_id=1, source_target_pairs={{0,1},{1,2},{2,3},{3,4},{4,5},{5,6},{6,7},{7,8},{8,9},{9,10},{10,1... | collective-permute-start | bytes 49160 | tf_op jit(solution)/shard_map/ppermute | solution.py:23
  235.5 14.2 %collective-permute-start.18 = (f32[4,1024]{1,0:T(4,128)S(1)}, f32[4,1024]{1,0:T(4,128)S(1)}, u32[]{:S(2)}, u32[]{:S(2)}) collective-permute-start(f32[4,1024]{1,0:T(4,128)S(1)} %get-tuple-element.34), channel_id=1, source_target_pairs={{2,0},{3,1},{4,2},{5,3},{6,4},{7,5},{8,6},{9,7},{10,8},{11,9},{12,... | collective-permute-start | bytes 49160 | tf_op jit(solution)/shard_map/ppermute | solution.py:23
  236.8 17.5 %collective-permute-start.19 = (f32[4,1024]{1,0:T(4,128)S(1)}, f32[4,1024]{1,0:T(4,128)S(1)}, u32[]{:S(2)}, u32[]{:S(2)}) collective-permute-start(f32[4,1024]{1,0:T(4,128)S(1)} %get-tuple-element.34), channel_id=1, source_target_pairs={{0,2},{1,3},{2,4},{3,5},{4,6},{5,7},{6,8},{7,9},{8,10},{9,11},{10,... | collective-permute-start | bytes 49160 | tf_op jit(solution)/shard_map/ppermute | solution.py:23
  241.4 12.9 %collective-permute-start.20 = (f32[4,1024]{1,0:T(4,128)S(1)}, f32[4,1024]{1,0:T(4,128)S(1)}, u32[]{:S(2)}, u32[]{:S(2)}) collective-permute-start(f32[4,1024]{1,0:T(4,128)S(1)} %get-tuple-element.34), channel_id=1, source_target_pairs={{3,0},{4,1},{5,2},{6,3},{7,4},{8,5},{9,6},{10,7},{11,8},{12,9},{13... | collective-permute-start | bytes 49160 | tf_op jit(solution)/shard_map/ppermute | solution.py:23
  242.7 11.6 %collective-permute-start.21 = (f32[4,1024]{1,0:T(4,128)S(1)}, f32[4,1024]{1,0:T(4,128)S(1)}, u32[]{:S(2)}, u32[]{:S(2)}) collective-permute-start(f32[4,1024]{1,0:T(4,128)S(1)} %get-tuple-element.34), channel_id=1, source_target_pairs={{0,3},{1,4},{2,5},{3,6},{4,7},{5,8},{6,9},{7,10},{8,11},{9,12},{10... | collective-permute-start | bytes 49160 | tf_op jit(solution)/shard_map/ppermute | solution.py:23
  248.4 5.9 %collective-permute-start.22 = (f32[4,1024]{1,0:T(4,128)S(1)}, f32[4,1024]{1,0:T(4,128)S(1)}, u32[]{:S(2)}, u32[]{:S(2)}) collective-permute-start(f32[4,1024]{1,0:T(4,128)S(1)} %get-tuple-element.34), channel_id=1, source_target_pairs={{4,0},{5,1},{6,2},{7,3},{8,4},{9,5},{10,6},{11,7},{12,8},{13,9},{1... | collective-permute-start | bytes 49160 | tf_op jit(solution)/shard_map/ppermute | solution.py:23
  249.7 6.0 %collective-permute-start.23 = (f32[4,1024]{1,0:T(4,128)S(1)}, f32[4,1024]{1,0:T(4,128)S(1)}, u32[]{:S(2)}, u32[]{:S(2)}) collective-permute-start(f32[4,1024]{1,0:T(4,128)S(1)} %get-tuple-element.34), channel_id=1, source_target_pairs={{0,4},{1,5},{2,6},{3,7},{4,8},{5,9},{6,10},{7,11},{8,12},{9,13},{1... | collective-permute-start | bytes 49160 | tf_op jit(solution)/shard_map/ppermute | solution.py:23
  255.8 11.5 %collective-permute-start.24 = (f32[4,1024]{1,0:T(4,128)S(1)}, f32[4,1024]{1,0:T(4,128)S(1)}, u32[]{:S(2)}, u32[]{:S(2)}) collective-permute-start(f32[4,1024]{1,0:T(4,128)S(1)} %add_divide_fusion.6), channel_id=1, source_target_pairs={{1,0},{2,1},{3,2},{4,3},{5,4},{6,5},{7,6},{8,7},{9,8},{10,9},{11,1... | collective-permute-start | bytes 49160 | tf_op jit(solution)/shard_map/ppermute | solution.py:23
  257.1 16.1 %collective-permute-start.25 = (f32[4,1024]{1,0:T(4,128)S(1)}, f32[4,1024]{1,0:T(4,128)S(1)}, u32[]{:S(2)}, u32[]{:S(2)}) collective-permute-start(f32[4,1024]{1,0:T(4,128)S(1)} %add_divide_fusion.6), channel_id=1, source_target_pairs={{0,1},{1,2},{2,3},{3,4},{4,5},{5,6},{6,7},{7,8},{8,9},{9,10},{10,1... | collective-permute-start | bytes 49160 | tf_op jit(solution)/shard_map/ppermute | solution.py:23
  260.1 14.3 %collective-permute-start.26 = (f32[4,1024]{1,0:T(4,128)S(1)}, f32[4,1024]{1,0:T(4,128)S(1)}, u32[]{:S(2)}, u32[]{:S(2)}) collective-permute-start(f32[4,1024]{1,0:T(4,128)S(1)} %add_divide_fusion.6), channel_id=1, source_target_pairs={{2,0},{3,1},{4,2},{5,3},{6,4},{7,5},{8,6},{9,7},{10,8},{11,9},{12,... | collective-permute-start | bytes 49160 | tf_op jit(solution)/shard_map/ppermute | solution.py:23
  261.4 17.6 %collective-permute-start.27 = (f32[4,1024]{1,0:T(4,128)S(1)}, f32[4,1024]{1,0:T(4,128)S(1)}, u32[]{:S(2)}, u32[]{:S(2)}) collective-permute-start(f32[4,1024]{1,0:T(4,128)S(1)} %add_divide_fusion.6), channel_id=1, source_target_pairs={{0,2},{1,3},{2,4},{3,5},{4,6},{5,7},{6,8},{7,9},{8,10},{9,11},{10,... | collective-permute-start | bytes 49160 | tf_op jit(solution)/shard_map/ppermute | solution.py:23
  266.0 13.1 %collective-permute-start.28 = (f32[4,1024]{1,0:T(4,128)S(1)}, f32[4,1024]{1,0:T(4,128)S(1)}, u32[]{:S(2)}, u32[]{:S(2)}) collective-permute-start(f32[4,1024]{1,0:T(4,128)S(1)} %add_divide_fusion.6), channel_id=1, source_target_pairs={{3,0},{4,1},{5,2},{6,3},{7,4},{8,5},{9,6},{10,7},{11,8},{12,9},{13... | collective-permute-start | bytes 49160 | tf_op jit(solution)/shard_map/ppermute | solution.py:23
  267.3 11.8 %collective-permute-start.29 = (f32[4,1024]{1,0:T(4,128)S(1)}, f32[4,1024]{1,0:T(4,128)S(1)}, u32[]{:S(2)}, u32[]{:S(2)}) collective-permute-start(f32[4,1024]{1,0:T(4,128)S(1)} %add_divide_fusion.6), channel_id=1, source_target_pairs={{0,3},{1,4},{2,5},{3,6},{4,7},{5,8},{6,9},{7,10},{8,11},{9,12},{10... | collective-permute-start | bytes 49160 | tf_op jit(solution)/shard_map/ppermute | solution.py:23
  273.2 5.9 %collective-permute-start.30 = (f32[4,1024]{1,0:T(4,128)S(1)}, f32[4,1024]{1,0:T(4,128)S(1)}, u32[]{:S(2)}, u32[]{:S(2)}) collective-permute-start(f32[4,1024]{1,0:T(4,128)S(1)} %add_divide_fusion.6), channel_id=1, source_target_pairs={{4,0},{5,1},{6,2},{7,3},{8,4},{9,5},{10,6},{11,7},{12,8},{13,9},{1... | collective-permute-start | bytes 49160 | tf_op jit(solution)/shard_map/ppermute | solution.py:23
  274.5 6.0 %collective-permute-start.31 = (f32[4,1024]{1,0:T(4,128)S(1)}, f32[4,1024]{1,0:T(4,128)S(1)}, u32[]{:S(2)}, u32[]{:S(2)}) collective-permute-start(f32[4,1024]{1,0:T(4,128)S(1)} %add_divide_fusion.6), channel_id=1, source_target_pairs={{0,4},{1,5},{2,6},{3,7},{4,8},{5,9},{6,10},{7,11},{8,12},{9,13},{1... | collective-permute-start | bytes 49160 | tf_op jit(solution)/shard_map/ppermute | solution.py:23
  280.5 12.0 %collective-permute-start.32 = (f32[4,1024]{1,0:T(4,128)S(1)}, f32[4,1024]{1,0:T(4,128)S(1)}, u32[]{:S(2)}, u32[]{:S(2)}) collective-permute-start(f32[4,1024]{1,0:T(4,128)S(1)} %add_divide_fusion.5), channel_id=1, source_target_pairs={{1,0},{2,1},{3,2},{4,3},{5,4},{6,5},{7,6},{8,7},{9,8},{10,9},{11,1... | collective-permute-start | bytes 49160 | tf_op jit(solution)/shard_map/ppermute | solution.py:23
  281.8 16.1 %collective-permute-start.33 = (f32[4,1024]{1,0:T(4,128)S(1)}, f32[4,1024]{1,0:T(4,128)S(1)}, u32[]{:S(2)}, u32[]{:S(2)}) collective-permute-start(f32[4,1024]{1,0:T(4,128)S(1)} %add_divide_fusion.5), channel_id=1, source_target_pairs={{0,1},{1,2},{2,3},{3,4},{4,5},{5,6},{6,7},{7,8},{8,9},{9,10},{10,1... | collective-permute-start | bytes 49160 | tf_op jit(solution)/shard_map/ppermute | solution.py:23
  284.9 14.3 %collective-permute-start.34 = (f32[4,1024]{1,0:T(4,128)S(1)}, f32[4,1024]{1,0:T(4,128)S(1)}, u32[]{:S(2)}, u32[]{:S(2)}) collective-permute-start(f32[4,1024]{1,0:T(4,128)S(1)} %add_divide_fusion.5), channel_id=1, source_target_pairs={{2,0},{3,1},{4,2},{5,3},{6,4},{7,5},{8,6},{9,7},{10,8},{11,9},{12,... | collective-permute-start | bytes 49160 | tf_op jit(solution)/shard_map/ppermute | solution.py:23
  286.2 17.6 %collective-permute-start.35 = (f32[4,1024]{1,0:T(4,128)S(1)}, f32[4,1024]{1,0:T(4,128)S(1)}, u32[]{:S(2)}, u32[]{:S(2)}) collective-permute-start(f32[4,1024]{1,0:T(4,128)S(1)} %add_divide_fusion.5), channel_id=1, source_target_pairs={{0,2},{1,3},{2,4},{3,5},{4,6},{5,7},{6,8},{7,9},{8,10},{9,11},{10,... | collective-permute-start | bytes 49160 | tf_op jit(solution)/shard_map/ppermute | solution.py:23
  291.2 12.6 %collective-permute-start.36 = (f32[4,1024]{1,0:T(4,128)S(1)}, f32[4,1024]{1,0:T(4,128)S(1)}, u32[]{:S(2)}, u32[]{:S(2)}) collective-permute-start(f32[4,1024]{1,0:T(4,128)S(1)} %add_divide_fusion.5), channel_id=1, source_target_pairs={{3,0},{4,1},{5,2},{6,3},{7,4},{8,5},{9,6},{10,7},{11,8},{12,9},{13... | collective-permute-start | bytes 49160 | tf_op jit(solution)/shard_map/ppermute | solution.py:23
  292.5 11.3 %collective-permute-start.37 = (f32[4,1024]{1,0:T(4,128)S(1)}, f32[4,1024]{1,0:T(4,128)S(1)}, u32[]{:S(2)}, u32[]{:S(2)}) collective-permute-start(f32[4,1024]{1,0:T(4,128)S(1)} %add_divide_fusion.5), channel_id=1, source_target_pairs={{0,3},{1,4},{2,5},{3,6},{4,7},{5,8},{6,9},{7,10},{8,11},{9,12},{10... | collective-permute-start | bytes 49160 | tf_op jit(solution)/shard_map/ppermute | solution.py:23
  297.9 5.9 %collective-permute-start.38 = (f32[4,1024]{1,0:T(4,128)S(1)}, f32[4,1024]{1,0:T(4,128)S(1)}, u32[]{:S(2)}, u32[]{:S(2)}) collective-permute-start(f32[4,1024]{1,0:T(4,128)S(1)} %add_divide_fusion.5), channel_id=1, source_target_pairs={{4,0},{5,1},{6,2},{7,3},{8,4},{9,5},{10,6},{11,7},{12,8},{13,9},{1... | collective-permute-start | bytes 49160 | tf_op jit(solution)/shard_map/ppermute | solution.py:23
  299.2 6.0 %collective-permute-start.39 = (f32[4,1024]{1,0:T(4,128)S(1)}, f32[4,1024]{1,0:T(4,128)S(1)}, u32[]{:S(2)}, u32[]{:S(2)}) collective-permute-start(f32[4,1024]{1,0:T(4,128)S(1)} %add_divide_fusion.5), channel_id=1, source_target_pairs={{0,4},{1,5},{2,6},{3,7},{4,8},{5,9},{6,10},{7,11},{8,12},{9,13},{1... | collective-permute-start | bytes 49160 | tf_op jit(solution)/shard_map/ppermute | solution.py:23
  (7 other events, 11.3 us)
where the time goes:
time: 310 us; the launch traced here: 306 us
  starting transfers between devices  107 us (35%)
  local copies, waits for them, and re-layouts  101 us (33%)
  other arithmetic  38 us (12%)
  waiting for transfers between devices  22 us (7%)
  blocking collectives  17.8 us (6%)
  matrix products  16 us (5%)
  between operations  4.27 us (1%)
    ppermute x40, starting transfers between devices, shifted(): lax.ppermute(value, axis, [(source, source + steps) for source in range(f...  107 us
    unnamed x40, local copies, waits for them, and re-layouts  49.5 us
    reduce_sum x13, other arithmetic, multilook(): values.reshape(row_count // ML_AZ, ML_AZ, blocks, 2, groups, ML_RG)  22.1 us
    ppermute x40, waiting for transfers between devices, shifted(): lax.ppermute(value, axis, [(source, source + steps) for source in range(f...  22 us
    all_gather x1, blocking collectives, prefix(): gathered = lax.all_gather(part, axis)  17.8 us
    slice x4, local copies, waits for them, and re-layouts, local(): partner_imag = partner[:, :, :, 1].astype(jnp.float32)  16.8 us
    dot_general x5, matrix products, split_bands(): filtered = jnp.dot(windows, matrix, preferred_element_type=jnp.float32)  13.2 us
    reshape x5, local copies, waits for them, and re-layouts, split_bands(): return filtered.astype(jnp.bfloat16).reshape(row_count, blocks, 2, 2, 128)  12.7 us
  transfers between devices with their start and end apart: 40, of which 5 were waited for; matrix products, arithmetic and copies ran while one was open for 30% of the time, Pallas kernels for 0%

commit v1 on v0

v1 whole, which is shorter than its diff:
```python
import jax
import jax.numpy as jnp
from jax import lax
from jax.experimental import pallas as pl
from jax.experimental.pallas import tpu as pltpu
from jax.sharding import PartitionSpec as P

TAPS = 32
ML_AZ = 4
ML_RG = 16
SPAN = 4
RADIUS = 8
ITERS = 4
LANES = 128
CELLS = LANES // ML_RG

eps_power = 1e-06
floor_weight = 0.1
ridge_weight = 0.05
split_coef = 2.0


def iota(shape, axis):
    return lax.broadcasted_iota(jnp.int32, shape, axis)


def back(x, steps):
    return pltpu.roll(x, LANES - steps, 1)


def group_sums(x0, x1, x2, x3):
    lane = iota((8, LANES), 1)
    even = lane % 2 == 0
    low = lane % 4 < 2
    u = jnp.where(even, x0 + back(x0, 1), x1 + pltpu.roll(x1, 1, 1))
    v = jnp.where(even, x2 + back(x2, 1), x3 + pltpu.roll(x3, 1, 1))
    return jnp.where(low, u + back(u, 2), v + pltpu.roll(v, 2, 1))


def pick4(x0, x1, x2, x3):
    lane = iota((8, LANES), 1) % 4
    return jnp.where(lane < 2, jnp.where(lane == 0, x0, x1), jnp.where(lane == 2, x2, x3))


def fill_filter(taps_ref, m_ref):
    width = 2 * LANES
    sub = iota((CELLS, width), 0)

    def placed(row):
        taps = jnp.broadcast_to(taps_ref[row : row + 1, :], (CELLS, width))
        result = jnp.zeros((CELLS, width), jnp.float32)
        for c in range(CELLS):
            result = jnp.where(sub == c, pltpu.roll(taps, (ML_RG * c - TAPS // 2) % width, 1), result)
        return result

    def along(base, j):
        both = [base if jj == 0 else pltpu.roll(base, jj, 1) for jj in (j, j + 1)]
        return jnp.concatenate(both, axis=0)

    for band in range(2):
        real, imag = placed(2 * band), placed(2 * band + 1)
        for j in range(0, ML_RG, 2):
            tr, ti = along(real, j), along(imag, j)
            real_row = ((band * 2 + 0) * ML_RG + j) * CELLS
            imag_row = ((band * 2 + 1) * ML_RG + j) * CELLS
            m_ref[real_row : real_row + 16, :width] = tr.astype(jnp.bfloat16)
            m_ref[real_row : real_row + 16, width:] = (-ti).astype(jnp.bfloat16)
            m_ref[imag_row : imag_row + 16, :width] = ti.astype(jnp.bfloat16)
            m_ref[imag_row : imag_row + 16, width:] = tr.astype(jnp.bfloat16)


def row_of(band, part, j):
    start = ((band * 2 + part) * ML_RG + j) * CELLS
    return slice(start, start + CELLS)


def apply_filter(matrix, windows):
    bands = lax.dot_general(
        matrix, windows, (((1,), (1,)), ((), ())), preferred_element_type=jnp.float32
    )
    return bands.astype(jnp.bfloat16).astype(jnp.float32)


def power_of(b_ref, d, band):
    total = jnp.zeros((CELLS, LANES), jnp.float32)
    for j in range(ML_RG):
        r = b_ref[d, row_of(band, 0, j)]
        i = b_ref[d, row_of(band, 1, j)]
        total = total + (r * r + i * i)
    return group_sums(total, total, total, total)


def weigh(cross, own, partner, flags):
    (re0, im0), (re1, im1) = cross
    pow0 = own[0] * partner[0] + eps_power
    pow1 = own[1] * partner[1] + eps_power
    coherence = (re0 * re0 + im0 * im0) / pow0 + (re1 * re1 + im1 * im1) / pow1
    weight = flags * 0.5 * coherence
    raw = split_coef * (im0 * re1 - re0 * im1) / jnp.sqrt(pow0 * pow1)
    return weight, weight * raw


def cell_sums(x):
    sub = iota((CELLS, LANES), 0)
    upto = x
    for step in (1, 2, 4):
        upto = upto + jnp.where(sub >= step, pltpu.roll(upto, step, 0), 0.0)
    total = jnp.broadcast_to(upto[CELLS - 1 : CELLS], (CELLS, LANES))
    return upto, total - upto + x, total


def solve_kernel(
    taps_ref, y_ref, out_ref, m_ref, b_ref, wh_ref, hb_ref, pw_ref, fl_ref, fh_ref, q_ref, s_ref, bt_ref, x_ref
):
    n, _, rows, _ = y_ref.shape
    lanes = rows - 4 * ML_AZ
    halos = hb_ref.shape[0]
    lane = iota((8, LANES), 1)
    sub = iota((8, LANES), 0)
    zero = jnp.zeros((8, LANES), jnp.float32)
    fill_filter(taps_ref, m_ref)

    def filtered(d, carry):
        windows, edges = [], []
        for part in range(2):
            v = y_ref[d, part].astype(jnp.float32).reshape(rows // 8, 8, LANES)
            subs = iota((rows // 8 - 1, 8, LANES), 1)
            merged = pltpu.roll(jnp.where(subs < 4, v[1:], v[:-1]), 4, 1)
            wide = iota((rows // 8 - 2, 8, LANES), 2)
            edge = jnp.where(wide < LANES // 2, merged[1:], merged[:-1])
            windows.append(v[1:-1].reshape(lanes, LANES))
            windows.append(edge.reshape(lanes, LANES))
            first, second, before, final = v[0], v[1], v[rows // 8 - 2], v[rows // 8 - 1]
            later = pltpu.roll(jnp.where(sub < 4, second, final), 4, 0)
            sooner = pltpu.roll(jnp.where(sub < 4, first, before), 4, 0)
            edges.append(jnp.where(sub < 4, final, first))
            edges.append(jnp.where(lane < LANES // 2, later, sooner))
            if part == 0:
                main = final[4:5]
                main = jnp.where(lane[:1] < LANES // 2, pltpu.roll(main, LANES // 2, 1), main)
                fl_ref[d] = jnp.broadcast_to(main, (8, LANES))
                side = first[0:1]
                side = jnp.where(lane[:1] < LANES // 2, side, pltpu.roll(side, LANES // 2, 1))
                fh_ref[d // 16] = jnp.where(lane // 8 == d % 16, jnp.broadcast_to(side, (8, LANES)), fh_ref[d // 16])
        windows = jnp.concatenate(windows, axis=1)
        if lanes < LANES:
            windows = jnp.concatenate([windows, jnp.zeros((LANES - lanes, 4 * LANES), jnp.float32)], axis=0)
        wh_ref[d] = jnp.concatenate(edges, axis=1)
        b_ref[d] = apply_filter(m_ref[...], windows.astype(jnp.bfloat16))
        for band in range(2):
            pw_ref[d, band] = power_of(b_ref, d, band)
        return carry

    lax.fori_loop(0, n, filtered, 0)

    for h in range(halos):
        hb_ref[h] = apply_filter(m_ref[...], wh_ref[16 * h : 16 * h + 16].reshape(LANES, 4 * LANES).astype(jnp.bfloat16))

    def pairs(d, carry):
        later = [jnp.minimum(d + k, n - 1) for k in range(1, SPAN + 1)]
        cross, partner = [], []
        for band in range(2):
            real = [zero] * SPAN
            imag = [zero] * SPAN
            for j in range(ML_RG):
                r = b_ref[d, row_of(band, 0, j)]
                i = b_ref[d, row_of(band, 1, j)]
                for k in range(SPAN):
                    pr = b_ref[later[k], row_of(band, 0, j)]
                    pi = b_ref[later[k], row_of(band, 1, j)]
                    real[k] = real[k] + (r * pr + i * pi)
                    imag[k] = imag[k] + (i * pr - r * pi)
            cross.append((group_sums(*real), group_sums(*imag)))
            partner.append(pick4(*[pw_ref[e, band] for e in later]))
        own = [pw_ref[d, band] for band in range(2)]
        weight, weighted = weigh(cross, own, partner, fl_ref[d])
        q_ref[0, d] = weight
        q_ref[1, d] = weighted
        return carry

    lax.fori_loop(0, n, pairs, 0)

    edge_sums = []
    hpow = [[power_of(hb_ref, h, band) for band in range(2)] for h in range(halos)]
    for h in range(halos):
        after = min(h + 1, halos - 1)

        def shifted(value, value_after, k):
            moved = back(value, 8 * k)
            if after == h:
                return moved
            return jnp.where(lane < LANES - 8 * k, moved, back(value_after, 8 * k))

        cross, partner = [], []
        for band in range(2):
            real = [zero] * SPAN
            imag = [zero] * SPAN
            for j in range(ML_RG):
                r = hb_ref[h, row_of(band, 0, j)]
                i = hb_ref[h, row_of(band, 1, j)]
                ra = hb_ref[after, row_of(band, 0, j)]
                ia = hb_ref[after, row_of(band, 1, j)]
                for k in range(SPAN):
                    pr = shifted(r, ra, k + 1)
                    pi = shifted(i, ia, k + 1)
                    real[k] = real[k] + (r * pr + i * pi)
                    imag[k] = imag[k] + (i * pr - r * pi)
            cross.append((group_sums(*real), group_sums(*imag)))
            partner.append(pick4(*[shifted(hpow[h][band], hpow[after][band], k) for k in range(1, SPAN + 1)]))
        weight, weighted = weigh(cross, hpow[h], partner, fh_ref[h])
        for which, value in enumerate((weight, weighted)):
            upto, onward, _ = cell_sums(value)
            wh_ref[h, :, which * 256 : which * 256 + 128] = upto
            wh_ref[h, :, which * 256 + 128 : which * 256 + 256] = onward

    for d in range(SPAN):
        x_ref[0, d] = zero
        x_ref[1, d] = zero
        x_ref[0, n + SPAN + d] = zero
        x_ref[1, n + SPAN + d] = zero
        for k in range(SPAN):
            s_ref[0, d, k] = zero
            s_ref[1, d, k] = zero

    def smooth(d, chain):
        h, place = d // 16, 8 * (d % 16)
        boxes = []
        for which in range(2):
            upto, onward, total = cell_sums(q_ref[which, d])
            far_upto = pltpu.roll(wh_ref[h, :, which * 256 : which * 256 + 128], (lanes - 4 - place) % LANES, 1)
            far_onward = pltpu.roll(wh_ref[h, :, which * 256 + 128 : which * 256 + 256], (LANES - 4 - place) % LANES, 1)
            sooner = jnp.where(lane < 4, far_onward, pltpu.roll(onward, 4, 1))
            later = jnp.where(lane >= lanes - 4, far_upto, back(upto, 4))
            boxes.append(total + sooner + later)
        phase = boxes[1] / (boxes[0] + floor_weight)
        weight = boxes[0] * (1.0 / (2 * RADIUS + 1))
        product = weight * phase
        total_weight = zero
        pull = ridge_weight * chain
        for k in range(SPAN):
            s = weight if k == 0 else back(weight, k)
            g = product if k == 0 else back(product, k)
            s_ref[0, d + SPAN, k] = s
            s_ref[1, d + SPAN, k] = g
            total_weight = total_weight + s + s_ref[0, d + SPAN - 1 - k, k]
            pull = pull - g + s_ref[1, d + SPAN - 1 - k, k]
        x_ref[0, d + SPAN] = chain
        bt_ref[0, d] = pull
        bt_ref[1, d] = 1.0 / (total_weight + ridge_weight)
        out_ref[d] = pltpu.roll(total_weight, 1, 1)
        return chain + phase

    lax.fori_loop(0, n, smooth, zero)

    for sweep in range(ITERS):
        old, new = sweep % 2, (sweep + 1) % 2

        def relax(d, carry):
            total = bt_ref[0, d]
            for k in range(SPAN):
                total = total + s_ref[0, d + SPAN, k] * x_ref[old, d + SPAN + 1 + k]
                total = total + s_ref[0, d + SPAN - 1 - k, k] * x_ref[old, d + SPAN - 1 - k]
            value = total * bt_ref[1, d]
            x_ref[new, d + SPAN] = value
            if sweep == ITERS - 1:
                out_ref[d] = jnp.where(lane % 4 == 1, out_ref[d], value)
            return carry

        lax.fori_loop(0, n, relax, 0)


def spread(scene, flags, looks, parts):
    width = scene.shape[2] // parts
    margin = 2 * LANES
    padded = jnp.pad(scene, ((0, 0), (0, 0), (margin, margin)))
    cut = jnp.stack([padded[:, :, width * q : width * (q + 1) + 2 * margin] for q in range(parts)])
    blocks = width // LANES + 4
    cut = cut.reshape(parts, 2, looks, ML_AZ, blocks, LANES).transpose(0, 2, 1, 4, 3, 5)
    shape = cut.shape
    q, block, place = iota(shape, 0), iota(shape, 3), iota(shape, 5)
    pattern = jnp.tile(flags.astype(cut.dtype), LANES // SPAN)
    inside = jnp.where(place // SPAN % 2 == 0, q < parts - 1, q > 0)
    cut = jnp.where((block == blocks - 1) & (place >= LANES // 2), pattern, cut)
    halo_pattern = jnp.where(inside, pattern, jnp.zeros_like(pattern))
    cut = jnp.where((block == 0) & (place < LANES // 2), halo_pattern, cut)
    return cut.reshape(parts * looks, 2, blocks * ML_AZ, LANES)


def local(slc_stack, band_taps, pair_flags):
    n = lax.axis_size("date")
    looks = slc_stack.shape[2] // ML_AZ
    parts = n // looks
    chunks = spread(slc_stack[0], pair_flags[0], looks, parts)
    rows = chunks.shape[2]
    lanes = rows - 4 * ML_AZ
    taps = jnp.pad(band_taps.astype(jnp.float32).reshape(4, TAPS), ((0, 0), (0, 2 * LANES - TAPS)))
    y = lax.all_to_all(chunks, "date", 0, 0, tiled=True)
    halos = n * 8 // LANES
    tile = (8, LANES)
    solved = pl.pallas_call(
        solve_kernel,
        out_shape=jax.ShapeDtypeStruct((n, *tile), jnp.float32),
        in_specs=[pl.BlockSpec(memory_space=pltpu.VMEM)] * 2,
        out_specs=pl.BlockSpec(memory_space=pltpu.VMEM),
        scratch_shapes=[
            pltpu.VMEM((4 * LANES, 4 * LANES), jnp.bfloat16),
            pltpu.VMEM((n, 4 * LANES, LANES), jnp.float32),
            pltpu.VMEM((n, 8, 4 * LANES), jnp.float32),
            pltpu.VMEM((halos, 4 * LANES, LANES), jnp.float32),
            pltpu.VMEM((n, 2, *tile), jnp.float32),
            pltpu.VMEM((n, *tile), jnp.float32),
            pltpu.VMEM((halos, *tile), jnp.float32),
            pltpu.VMEM((2, n, *tile), jnp.float32),
            pltpu.VMEM((2, n + SPAN, SPAN, *tile), jnp.float32),
            pltpu.VMEM((2, n, *tile), jnp.float32),
            pltpu.VMEM((2, n + 2 * SPAN, *tile), jnp.float32),
        ],
        compiler_params=pltpu.CompilerParams(vmem_limit_bytes=60 * 1024 * 1024),
    )(taps, y)
    z = lax.all_to_all(solved, "date", 0, 0, tiled=True)
    z = z[:, :, :lanes].reshape(parts, looks, 8, lanes // 4, 4)[..., :2]
    z = z.transpose(4, 1, 0, 3, 2).reshape(2, 1, looks, parts * lanes * 2)
    return (z[0], z[1])


def solution(mesh):
    in_specs = (P("date", None, "group", None), P(), P("date", None))
    out_specs = (P("date", "group", None), P("date", "group", None))
    return jax.shard_map(local, mesh=mesh, in_specs=in_specs, out_specs=out_specs, check_vma=False)
```

time: 310 us -> 75.6 us (0.24); the launches traced: 306 us -> 75.3 us
  starting transfers between devices: 107 us -> 7.52 us
  local copies, waits for them, and re-layouts: 101 us -> 7.26 us
  other arithmetic: 38 us -> 1.17 us
  Pallas kernels: 0 us -> 19.6 us
  matrix products: 16 us -> 0 us
  between operations: 4.27 us -> 0.79 us
  blocking collectives: 17.8 us -> 14.4 us
    ppermute x40 -> x0, starting transfers between devices: 107 us -> none  [shifted(): lax.ppermute(value, axis, [(source, source + steps) for source in range(f...]
    unnamed x40 -> x6, local copies, waits for them, and re-layouts: 49.5 us -> 1.03 us
    all_to_all x0 -> x1, waiting for transfers between devices: none -> 24.5 us  [local(): y = lax.all_to_all(chunks, 'date', 0, 0, tiled=True)]
    slice x11 -> x4, local copies, waits for them, and re-layouts: 24.7 us -> 1.9 us  [the longest x1 1.31 us: spread(): padded[:, :, width * q:width * (q + 1) + 2 * margin]]
    reduce_sum x13 -> x0, other arithmetic: 22.1 us -> none  [multilook(): values.reshape(row_count // ML_AZ, ML_AZ, blocks, 2, groups, ML_RG)]
    ppermute x40 -> x0, waiting for transfers between devices: 22 us -> none  [shifted(): lax.ppermute(value, axis, [(source, source + steps) for source in range(f...]
    pallas_call x0 -> x1, Pallas kernels: none -> 19.6 us  [local(): pl.pallas_call(solve_kernel, out_shape=jax.ShapeDtypeStruct((n, *tile), j...]
    all_gather x1 -> x0, blocking collectives: 17.8 us -> none  [prefix(): gathered = lax.all_gather(part, axis)]
  transfers between devices with their start and end apart: 40 -> 1, of which waited for: 5 -> 1; matrix products, arithmetic and copies ran while one was open for 30% -> 1% of each run, Pallas kernels for 0% -> 0%
where the time goes in v1:
time: 75.6 us; the launch traced here: 75.3 us
  waiting for transfers between devices  24.5 us (32%)
  Pallas kernels  19.6 us (26%)
  blocking collectives  14.4 us (19%)
  starting transfers between devices  7.52 us (10%)
  local copies, waits for them, and re-layouts  7.26 us (10%)
  other arithmetic  1.17 us (2%)
  between operations  0.79 us (1%)
    all_to_all x1, waiting for transfers between devices, local(): y = lax.all_to_all(chunks, 'date', 0, 0, tiled=True)  24.5 us
    pallas_call x1, Pallas kernels, local(): pl.pallas_call(solve_kernel, out_shape=jax.ShapeDtypeStruct((n, *tile), j...  19.6 us
    all_to_all x1, blocking collectives, local(): z = lax.all_to_all(solved, 'date', 0, 0, tiled=True)  14.4 us
    all_to_all x1, starting transfers between devices, local(): y = lax.all_to_all(chunks, 'date', 0, 0, tiled=True)  7.52 us
    squeeze x2, local copies, waits for them, and re-layouts, local(): return (z[0], z[1])  1.53 us
  transfers between devices with their start and end apart: 1, of which 1 were waited for; matrix products, arithmetic and copies ran while one was open for 1% of the time, Pallas kernels for 0%

profile of v1, /device:TPU:0, one launch (start us, length us, event | category | flops | bytes accessed | tf_op | source)
XLA Modules:
  0.0 75.3 jit_solution(18397882937436642065)
XLA Ops:
  0.7 1.3 %pad_slice_fusion.1 = (bf16[2,16,4608]{2,1,0:T(8,128)(2,1)S(1)}, bf16[2,16,4608]{2,1,0:T(8,128)(2,1)S(1)}, bf16[2,16,4608]{2,1,0:T(8,128)(2,1)S(1)}, bf16[2,16,4608]{2,1,0:T(8,128)(2,1)S(1)}) fusion(bf16[2,16,16384]{2,1,0:T(8,128)(2,1)} %bitcast.16), kind=kLoop, calls=%fused_computation.13 | loop fusion | bytes 2818048 | tf_op jit(solution)/shard_map/slice | solution.py:276
  2.0 0.0 copy-start.2
  2.0 0.2 stack.15
  2.2 0.2 stack.16
  2.4 0.2 stack.17
  2.6 0.2 stack.18
  2.7 0.0 copy-done.2
  2.8 0.1 tile.13
  2.9 0.5 and_select_fusion.1
  3.4 1.5 %copy.11 = bf16[4,4,2,36,4,128]{5,4,3,2,1,0:T(4,128)(2,1)} copy(bf16[4,4,2,36,4,128]{5,3,4,1,2,0:T(8,128)(2,1)S(1)} %and_select_fusion.1) | data formatting | bytes 2359296 | tf_op jit(solution)/shard_map/jit(_where)/select_n | solution.py:285
  4.9 0.0 copy-start.1
  4.9 7.5 %all-to-all-start = ((bf16[16,2,144,128]{3,2,1,0:T(8,128)(2,1)}), bf16[16,2,144,128]{3,2,1,0:T(8,128)(2,1)S(1)}, u32[]{:S(2)}, u32[]{:S(2)}) async-start(bf16[16,2,144,128]{3,2,1,0:T(8,128)(2,1)} %bitcast.4), calls=%async_computation | async-start | bytes 2359296 | tf_op jit(solution)/shard_map/all_to_all | solution.py:297
  12.4 0.0 copy-done.1
  12.4 0.6 pad_convert_fusion.taps_ref
  13.0 24.5 %all-to-all-done.y_ref = bf16[16,2,144,128]{3,2,1,0:T(8,128)(2,1)S(1)} async-done(((bf16[16,2,144,128]{3,2,1,0:T(8,128)(2,1)}), bf16[16,2,144,128]{3,2,1,0:T(8,128)(2,1)S(1)}, u32[]{:S(2)}, u32[]{:S(2)}) %all-to-all-start) | async-done | bytes 1179680 | tf_op jit(solution)/shard_map/all_to_all | solution.py:297
  37.6 0.0 copy-start
  37.6 1.0 %copy-done = bf16[16,2,144,128]{3,2,1,0:T(8,128)(2,1)} copy-done((bf16[16,2,144,128]{3,2,1,0:T(8,128)(2,1)}, bf16[16,2,144,128]{3,2,1,0:T(8,128)(2,1)S(1)}, u32[]{:S(2)}) %copy-start) | copy-done | bytes 1179672
  38.6 19.6 %shard_map.50 = f32[16,8,128]{2,1,0:T(8,128)} custom-call(f32[4,256]{1,0:T(4,128)} %pad_convert_fusion.taps_ref, bf16[16,2,144,128]{3,2,1,0:T(8,128)(2,1)} %copy-done), custom_call_target="tpu_custom_call" | custom-call | tf_op jit(solution)/shard_map/pallas_call | solution.py:300
  58.2 14.4 %all_to_all.10 = f32[16,8,128]{2,1,0:T(8,128)S(1)} all-to-all(f32[16,8,128]{2,1,0:T(8,128)} %shard_map.50), channel_id=1, replica_groups=mesh['group'=2,'date'=16] {'date'}, dimensions={0} | all-to-all | bytes 131072 | tf_op jit(solution)/shard_map/all_to_all | solution.py:320
  72.6 0.3 copy.12
  72.9 0.2 slice_bitcast_fusion
  73.1 0.6 fusion.4
  73.7 0.8 %squeeze.11 = f32[1,4,1024]{2,1,0:T(4,128)} reshape(f32[1,4,4,32,8]{4,3,2,1,0:T(8,128)S(1)} %copy.13) | data formatting | bytes 32768 | tf_op jit(solution)/shard_map/squeeze | solution.py:323
  74.5 0.8 %squeeze.12 = f32[1,4,1024]{2,1,0:T(4,128)} reshape(f32[1,4,4,32,8]{4,3,2,1,0:T(8,128)S(1)} %copy.14) | data formatting | bytes 32768 | tf_op jit(solution)/shard_map/squeeze | solution.py:323
  (9 shorter events, 0.1 us)
Async XLA Ops:
  2.0 0.7 copy-start.2
  4.9 7.5 %copy-start.1 = (bf16[2,2,32]{2,1,0:T(2,128)(2,1)S(1)}, bf16[2,2,32]{2,1,0:T(2,128)(2,1)}, u32[]{:S(2)}) copy-start(bf16[2,2,32]{2,1,0:T(2,128)(2,1)} %param.4) | copy-start | bytes 772
  4.9 32.7 %all-to-all-start = ((bf16[16,2,144,128]{3,2,1,0:T(8,128)(2,1)}), bf16[16,2,144,128]{3,2,1,0:T(8,128)(2,1)S(1)}, u32[]{:S(2)}, u32[]{:S(2)}) async-start(bf16[16,2,144,128]{3,2,1,0:T(8,128)(2,1)} %bitcast.4), calls=%async_computation | async-start | bytes 2359296 | tf_op jit(solution)/shard_map/all_to_all | solution.py:297
  37.6 1.0 %copy-start = (bf16[16,2,144,128]{3,2,1,0:T(8,128)(2,1)}, bf16[16,2,144,128]{3,2,1,0:T(8,128)(2,1)S(1)}, u32[]{:S(2)}) copy-start(bf16[16,2,144,128]{3,2,1,0:T(8,128)(2,1)S(1)} %all-to-all-done.y_ref) | copy-start | bytes 3538948

commit v2 on v1

--- a/solution.py
+++ b/solution.py
@@ -42,7 +42,7 @@
     return jnp.where(lane < 2, jnp.where(lane == 0, x0, x1), jnp.where(lane == 2, x2, x3))
 
 
-def fill_filter(taps_ref, m_ref):
+def filter_kernel(taps_ref, m_ref):
     width = 2 * LANES
     sub = iota((CELLS, width), 0)
 
@@ -110,7 +110,7 @@
 
 
 def solve_kernel(
-    taps_ref, y_ref, out_ref, m_ref, b_ref, wh_ref, hb_ref, pw_ref, fl_ref, fh_ref, q_ref, s_ref, bt_ref, x_ref
+    m_ref, y_ref, out_ref, b_ref, wh_ref, hb_ref, pw_ref, fl_ref, fh_ref, q_ref, s_ref, bt_ref, x_ref
 ):
     n, _, rows, _ = y_ref.shape
     lanes = rows - 4 * ML_AZ
@@ -118,7 +118,9 @@
     lane = iota((8, LANES), 1)
     sub = iota((8, LANES), 0)
     zero = jnp.zeros((8, LANES), jnp.float32)
-    fill_filter(taps_ref, m_ref)
+
+    def each(step, start):
+        return lax.fori_loop(0, n, step, start, unroll=n <= 16)
 
     def filtered(d, carry):
         windows, edges = [], []
@@ -151,7 +153,7 @@
             pw_ref[d, band] = power_of(b_ref, d, band)
         return carry
 
-    lax.fori_loop(0, n, filtered, 0)
+    each(filtered, 0)
 
     for h in range(halos):
         hb_ref[h] = apply_filter(m_ref[...], wh_ref[16 * h : 16 * h + 16].reshape(LANES, 4 * LANES).astype(jnp.bfloat16))
@@ -178,7 +180,7 @@
         q_ref[1, d] = weighted
         return carry
 
-    lax.fori_loop(0, n, pairs, 0)
+    each(pairs, 0)
 
     edge_sums = []
     hpow = [[power_of(hb_ref, h, band) for band in range(2)] for h in range(halos)]
@@ -250,7 +252,7 @@
         out_ref[d] = pltpu.roll(total_weight, 1, 1)
         return chain + phase
 
-    lax.fori_loop(0, n, smooth, zero)
+    each(smooth, zero)
 
     for sweep in range(ITERS):
         old, new = sweep % 2, (sweep + 1) % 2
@@ -266,44 +268,134 @@
                 out_ref[d] = jnp.where(lane % 4 == 1, out_ref[d], value)
             return carry
 
-        lax.fori_loop(0, n, relax, 0)
-
-
-def spread(scene, flags, looks, parts):
-    width = scene.shape[2] // parts
-    margin = 2 * LANES
-    padded = jnp.pad(scene, ((0, 0), (0, 0), (margin, margin)))
-    cut = jnp.stack([padded[:, :, width * q : width * (q + 1) + 2 * margin] for q in range(parts)])
-    blocks = width // LANES + 4
-    cut = cut.reshape(parts, 2, looks, ML_AZ, blocks, LANES).transpose(0, 2, 1, 4, 3, 5)
-    shape = cut.shape
-    q, block, place = iota(shape, 0), iota(shape, 3), iota(shape, 5)
-    pattern = jnp.tile(flags.astype(cut.dtype), LANES // SPAN)
-    inside = jnp.where(place // SPAN % 2 == 0, q < parts - 1, q > 0)
-    cut = jnp.where((block == blocks - 1) & (place >= LANES // 2), pattern, cut)
-    halo_pattern = jnp.where(inside, pattern, jnp.zeros_like(pattern))
-    cut = jnp.where((block == 0) & (place < LANES // 2), halo_pattern, cut)
-    return cut.reshape(parts * looks, 2, blocks * ML_AZ, LANES)
+        each(relax, 0)
+
+
+def spread_kernel(x_ref, flags_ref, out_ref, held_ref, made_ref, in_sems, out_sems):
+    parts = in_sems.shape[1]
+    looks = out_ref.shape[0] // parts
+    rows = out_ref.shape[2]
+    width = x_ref.shape[3] // parts
+    pairs = width // (2 * LANES)
+    sub = iota((8, LANES), 0)
+    lane = iota((8, LANES), 1)
+    flags = [flags_ref[0, k].astype(jnp.float32) for k in range(SPAN)]
+    pattern = jnp.where(
+        lane % 4 < 2, jnp.where(lane % 4 == 0, flags[0], flags[1]), jnp.where(lane % 4 == 2, flags[2], flags[3])
+    )
+    zero = jnp.zeros((8, LANES), jnp.float32)
+
+    def fetch(part, q):
+        columns = pl.ds(q * width, width)
+        return pltpu.make_async_copy(x_ref.at[0, part, :, columns], held_ref.at[part, :, columns], in_sems.at[part, q])
+
+    def send(part, q):
+        chunks = pl.ds(q * looks, looks)
+        return pltpu.make_async_copy(made_ref.at[chunks, part], out_ref.at[chunks, part], out_sems.at[part, q])
+
+    for part in range(2):
+        for q in range(parts):
+            fetch(part, q).start()
+    for part in range(2):
+        made = {}
+
+        def pair_of(index, half):
+            if index < 0 or index >= parts * pairs:
+                return zero, zero
+            if (index, half) not in made:
+                start = index * 2 * LANES
+                first = held_ref[part, :, start : start + LANES].astype(jnp.float32)[8 * half : 8 * half + 8]
+                second = held_ref[part, :, start + LANES : start + 2 * LANES].astype(jnp.float32)[8 * half : 8 * half + 8]
+                mixed = pltpu.roll(jnp.where(sub < 4, second, first), 4, 0)
+                made[index, half] = (jnp.where(sub < 4, first, mixed), jnp.where(sub < 4, mixed, second))
+            return made[index, half]
+
+        for q in range(parts):
+            if q == 0:
+                fetch(part, 0).wait()
+            if q + 1 < parts:
+                fetch(part, q + 1).wait()
+            for tile in range(rows // 16):
+                upper = q * pairs - 1 + 2 * tile
+                for half in range(looks // 2):
+                    for odd in range(2):
+                        top = pair_of(upper, half)[odd]
+                        bottom = pair_of(upper + 1, half)[odd]
+                        if part == 0 and tile == 0:
+                            side = lane // SPAN % 2
+                            inside = jnp.where(side == 0, float(q < parts - 1), float(q > 0))
+                            top = jnp.where((sub < 4) & (lane < LANES // 2), pattern * inside, top)
+                        if part == 0 and tile == rows // 16 - 1:
+                            bottom = jnp.where((sub >= 4) & (lane >= LANES // 2), pattern, bottom)
+                        both = jnp.concatenate([top, bottom], axis=0).astype(jnp.bfloat16)
+                        made_ref[q * looks + 2 * half + odd, part, 16 * tile : 16 * tile + 16, :] = both
+            send(part, q).start()
+    for part in range(2):
+        for q in range(parts):
+            send(part, q).wait()
+
+
+def gather_kernel(z_ref, phase_ref, weight_ref):
+    count = z_ref.shape[0]
+    looks = phase_ref.shape[1]
+    width = 2 * LANES
+    source = iota((LANES, 2 * width), 0)
+    column = iota((LANES, 2 * width), 1)
+    block = column % width // CELLS
+    chosen = (source == SPAN * block + column // width).astype(jnp.float32)
+    values = z_ref[...].reshape(count * CELLS, LANES)
+    moved = jnp.dot(values, chosen, precision=lax.Precision.HIGHEST, preferred_element_type=jnp.float32)
+    row = iota((count * CELLS, 2 * width), 0)
+    column = iota((count * CELLS, 2 * width), 1)
+    moved = jnp.where(row % CELLS == column % CELLS, moved, 0.0)
+    adder = (iota((count, count * CELLS), 1) // CELLS == iota((count, count * CELLS), 0)).astype(jnp.float32)
+    lines = jnp.dot(adder, moved, precision=lax.Precision.HIGHEST, preferred_element_type=jnp.float32)
+    for q in range(count // looks):
+        for which, out in enumerate((phase_ref, weight_ref)):
+            out[0, :, width * q : width * (q + 1)] = lines[
+                looks * q : looks * (q + 1), width * which : width * (which + 1)
+            ]
 
 
 def local(slc_stack, band_taps, pair_flags):
     n = lax.axis_size("date")
     looks = slc_stack.shape[2] // ML_AZ
     parts = n // looks
-    chunks = spread(slc_stack[0], pair_flags[0], looks, parts)
-    rows = chunks.shape[2]
-    lanes = rows - 4 * ML_AZ
-    taps = jnp.pad(band_taps.astype(jnp.float32).reshape(4, TAPS), ((0, 0), (0, 2 * LANES - TAPS)))
-    y = lax.all_to_all(chunks, "date", 0, 0, tiled=True)
+    lanes = slc_stack.shape[3] // (parts * LANES) * ML_AZ
+    rows = lanes + 4 * ML_AZ
     halos = n * 8 // LANES
     tile = (8, LANES)
+    in_vmem = pl.BlockSpec(memory_space=pltpu.VMEM)
+    anywhere = pl.BlockSpec(memory_space=pl.ANY)
+    params = pltpu.CompilerParams(vmem_limit_bytes=60 * 1024 * 1024)
+    chunks = pl.pallas_call(
+        spread_kernel,
+        out_shape=jax.ShapeDtypeStruct((n, 2, rows, LANES), jnp.bfloat16),
+        in_specs=[anywhere, pl.BlockSpec(memory_space=pltpu.SMEM)],
+        out_specs=anywhere,
+        scratch_shapes=[
+            pltpu.VMEM(slc_stack.shape[1:], jnp.bfloat16),
+            pltpu.VMEM((n, 2, rows, LANES), jnp.bfloat16),
+            pltpu.SemaphoreType.DMA((2, parts)),
+            pltpu.SemaphoreType.DMA((2, parts)),
+        ],
+        compiler_params=params,
+    )(slc_stack, pair_flags)
+    y = pltpu.with_memory_space_constraint(lax.all_to_all(chunks, "date", 0, 0, tiled=True), pltpu.VMEM)
+    taps = jnp.pad(band_taps.astype(jnp.float32).reshape(4, TAPS), ((0, 0), (0, 2 * LANES - TAPS)))
+    matrix = pl.pallas_call(
+        filter_kernel,
+        out_shape=jax.ShapeDtypeStruct((4 * LANES, 4 * LANES), jnp.bfloat16),
+        in_specs=[in_vmem],
+        out_specs=in_vmem,
+        compiler_params=params,
+    )(taps)
     solved = pl.pallas_call(
         solve_kernel,
         out_shape=jax.ShapeDtypeStruct((n, *tile), jnp.float32),
-        in_specs=[pl.BlockSpec(memory_space=pltpu.VMEM)] * 2,
-        out_specs=pl.BlockSpec(memory_space=pltpu.VMEM),
+        in_specs=[in_vmem, in_vmem],
+        out_specs=in_vmem,
         scratch_shapes=[
-            pltpu.VMEM((4 * LANES, 4 * LANES), jnp.bfloat16),
             pltpu.VMEM((n, 4 * LANES, LANES), jnp.float32),
             pltpu.VMEM((n, 8, 4 * LANES), jnp.float32),
             pltpu.VMEM((halos, 4 * LANES, LANES), jnp.float32),
@@ -315,11 +407,22 @@
             pltpu.VMEM((2, n, *tile), jnp.float32),
             pltpu.VMEM((2, n + 2 * SPAN, *tile), jnp.float32),
         ],
-        compiler_params=pltpu.CompilerParams(vmem_limit_bytes=60 * 1024 * 1024),
-    )(taps, y)
+        compiler_params=params,
+    )(matrix, y)
     z = lax.all_to_all(solved, "date", 0, 0, tiled=True)
-    z = z[:, :, :lanes].reshape(parts, looks, 8, lanes // 4, 4)[..., :2]
-    z = z.transpose(4, 1, 0, 3, 2).reshape(2, 1, looks, parts * lanes * 2)
+    shape = (1, looks, slc_stack.shape[3] // ML_RG)
+    if lanes == LANES:
+        return tuple(
+            pl.pallas_call(
+                gather_kernel,
+                out_shape=[jax.ShapeDtypeStruct(shape, jnp.float32)] * 2,
+                in_specs=[in_vmem],
+                out_specs=[in_vmem] * 2,
+                compiler_params=params,
+            )(z)
+        )
+    z = z[:, :, :lanes].reshape(parts, looks, CELLS, lanes // SPAN, SPAN)[..., :2]
+    z = z.transpose(4, 1, 0, 3, 2).reshape(2, *shape)
     return (z[0], z[1])
 
 

time: 75.6 us -> 59.4 us (0.79)
  local copies, waits for them, and re-layouts: 7.26 us -> 0.01 us
  Pallas kernels: 19.6 us -> 13.1 us
  waiting for transfers between devices: 24.5 us -> 22.7 us
    pallas_call x1, Pallas kernels: 19.6 us -> 6.28 us  [local(): pl.pallas_call(solve_kernel, out_shape=jax.ShapeDtypeStruct((n, *tile), j...]
    pallas_call x0 -> x3, Pallas kernels: none -> 6.83 us  [the longest x1 2.92 us: local(): pl.pallas_call(spread_kernel, out_shape=jax.ShapeDtypeStruct((n, 2, rows,...]
    slice x4 -> x0, local copies, waits for them, and re-layouts: 1.9 us -> none  [the longest x1 1.31 us: spread(): padded[:, :, width * q:width * (q + 1) + 2 * margin]]
    all_to_all x1, waiting for transfers between devices: 24.5 us -> 22.7 us  [local(): lax.all_to_all(chunks, 'date', 0, 0, tiled=True)]
    squeeze x2 -> x0, local copies, waits for them, and re-layouts: 1.53 us -> none  [local(): return (z[0], z[1])]
    select_n x1 -> x0, local copies, waits for them, and re-layouts: 1.48 us -> none  [spread(): cut = jnp.where((block == 0) & (place < LANES // 2), halo_pattern, cut)]
    unnamed x6 -> x2, local copies, waits for them, and re-layouts: 1.03 us -> 0.01 us
    another operation x6 -> x0, local copies, waits for them, and re-layouts: 0.81 us -> none  [the longest x4 0.69 us: spread(): jnp.stack([padded[:, :, width * q:width * (q + 1) + 2 * margin] for q in...]
  transfers between devices with their start and end apart: 1 -> 1, of which waited for: 1 -> 1; matrix products, arithmetic and copies ran while one was open for 1% -> 1% of each run, Pallas kernels for 0% -> 3%
where the time goes in v2:
time: 59.4 us; the launch traced here: 58.9 us
  waiting for transfers between devices  22.7 us (38%)
  blocking collectives  14.5 us (24%)
  Pallas kernels  13.1 us (22%)
  starting transfers between devices  7.4 us (12%)
  between operations  0.66 us (1%)
  other arithmetic  0.6 us (1%)
    all_to_all x1, waiting for transfers between devices, local(): lax.all_to_all(chunks, 'date', 0, 0, tiled=True)  22.7 us
    all_to_all x1, blocking collectives, local(): z = lax.all_to_all(solved, 'date', 0, 0, tiled=True)  14.5 us
    all_to_all x1, starting transfers between devices, local(): lax.all_to_all(chunks, 'date', 0, 0, tiled=True)  7.4 us
    pallas_call x1, Pallas kernels, local(): pl.pallas_call(solve_kernel, out_shape=jax.ShapeDtypeStruct((n, *tile), j...  6.28 us
    pallas_call x1, Pallas kernels, local(): pl.pallas_call(spread_kernel, out_shape=jax.ShapeDtypeStruct((n, 2, rows,...  2.92 us
    pallas_call x1, Pallas kernels, local(): pl.pallas_call(gather_kernel, out_shape=[jax.ShapeDtypeStruct(shape, jnp....  2.06 us
    pallas_call x1, Pallas kernels, local(): pl.pallas_call(filter_kernel, out_shape=jax.ShapeDtypeStruct((4 * LANES,...  1.86 us
  transfers between devices with their start and end apart: 1, of which 1 were waited for; matrix products, arithmetic and copies ran while one was open for 1% of the time, Pallas kernels for 3%

profile of v2, /device:TPU:0, one launch (start us, length us, event | category | flops | bytes accessed | tf_op | source)
XLA Modules:
  0.0 58.9 jit_solution(17337965212197990957)
XLA Ops:
  0.6 2.9 %shard_map.51 = bf16[16,2,144,128]{3,2,1,0:T(8,128)(2,1)} custom-call(bf16[1,2,16,16384]{3,2,1,0:T(8,128)(2,1)} %x_ref.1, s32[1,4]{1,0:T(1,128)} %flags_ref.1), custom_call_target="tpu_custom_call" | custom-call | tf_op jit(solution)/shard_map/pallas_call | solution.py:371
  3.6 0.0 copy-start
  3.6 7.4 %all-to-all-start = ((bf16[16,2,144,128]{3,2,1,0:T(8,128)(2,1)}), bf16[16,2,144,128]{3,2,1,0:T(8,128)(2,1)S(1)}, u32[]{:S(2)}, u32[]{:S(2)}) async-start(bf16[16,2,144,128]{3,2,1,0:T(8,128)(2,1)} %shard_map.51), calls=%async_computation | async-start | bytes 2359296 | tf_op jit(solution)/shard_map/all_to_all | solution.py:384
  11.0 0.0 copy-done
  11.0 0.6 %pad_convert_fusion.taps_ref = f32[4,256]{1,0:T(4,128)} fusion(bf16[4,32]{1,0:T(4,128)(2,1)S(1)} %bitcast.1), kind=kLoop, calls=%fused_computation | loop fusion | flops 1024 | bytes 4352 | tf_op jit(solution)/shard_map/jit(_pad)/pad | solution.py:385
  11.6 1.9 %shard_map.50.m_ref = bf16[512,512]{1,0:T(8,128)(2,1)} custom-call(f32[4,256]{1,0:T(4,128)} %pad_convert_fusion.taps_ref), custom_call_target="tpu_custom_call" | custom-call | tf_op jit(solution)/shard_map/pallas_call | solution.py:386
  13.4 22.7 %all-to-all-done.y_ref = bf16[16,2,144,128]{3,2,1,0:T(8,128)(2,1)S(1)} async-done(((bf16[16,2,144,128]{3,2,1,0:T(8,128)(2,1)}), bf16[16,2,144,128]{3,2,1,0:T(8,128)(2,1)S(1)}, u32[]{:S(2)}, u32[]{:S(2)}) %all-to-all-start) | async-done | bytes 1179680 | tf_op jit(solution)/shard_map/all_to_all | solution.py:384
  36.1 6.3 %shard_map.52 = f32[16,8,128]{2,1,0:T(8,128)} custom-call(bf16[512,512]{1,0:T(8,128)(2,1)} %shard_map.50.m_ref, bf16[16,2,144,128]{3,2,1,0:T(8,128)(2,1)S(1)} %all-to-all-done.y_ref), custom_call_target="tpu_custom_call" | custom-call | tf_op jit(solution)/shard_map/pallas_call | solution.py:393
  42.4 14.5 %all_to_all.10.z_ref = f32[16,8,128]{2,1,0:T(8,128)} all-to-all(f32[16,8,128]{2,1,0:T(8,128)} %shard_map.52), channel_id=1, replica_groups=mesh['group'=2,'date'=16] {'date'}, dimensions={0} | all-to-all | bytes 131072 | tf_op jit(solution)/shard_map/all_to_all | solution.py:412
  56.9 2.1 %shard_map.53 = (f32[1,4,1024]{2,1,0:T(4,128)}, f32[1,4,1024]{2,1,0:T(4,128)}) custom-call(f32[16,8,128]{2,1,0:T(8,128)} %all_to_all.10.z_ref), custom_call_target="tpu_custom_call" | custom-call | tf_op jit(solution)/shard_map/pallas_call | solution.py:416
Async XLA Ops:
  3.6 7.4 %copy-start = (bf16[2,2,32]{2,1,0:T(2,128)(2,1)S(1)}, bf16[2,2,32]{2,1,0:T(2,128)(2,1)}, u32[]{:S(2)}) copy-start(bf16[2,2,32]{2,1,0:T(2,128)(2,1)} %param.4) | copy-start | bytes 772
  3.6 32.5 %all-to-all-start = ((bf16[16,2,144,128]{3,2,1,0:T(8,128)(2,1)}), bf16[16,2,144,128]{3,2,1,0:T(8,128)(2,1)S(1)}, u32[]{:S(2)}, u32[]{:S(2)}) async-start(bf16[16,2,144,128]{3,2,1,0:T(8,128)(2,1)} %shard_map.51), calls=%async_computation | async-start | bytes 2359296 | tf_op jit(solution)/shard_map/all_to_all | solution.py:384

commit v3 on v2

--- a/solution.py
+++ b/solution.py
@@ -101,16 +101,16 @@
 
 
 def cell_sums(x):
-    sub = iota((CELLS, LANES), 0)
+    sub = iota(x.shape, 1)
     upto = x
     for step in (1, 2, 4):
-        upto = upto + jnp.where(sub >= step, pltpu.roll(upto, step, 0), 0.0)
-    total = jnp.broadcast_to(upto[CELLS - 1 : CELLS], (CELLS, LANES))
+        upto = upto + jnp.where(sub >= step, pltpu.roll(upto, step, 1), 0.0)
+    total = jnp.broadcast_to(upto[:, CELLS - 1 : CELLS], x.shape)
     return upto, total - upto + x, total
 
 
 def solve_kernel(
-    m_ref, y_ref, out_ref, b_ref, wh_ref, hb_ref, pw_ref, fl_ref, fh_ref, q_ref, s_ref, bt_ref, x_ref
+    m_ref, y_ref, out_ref, b_ref, wh_ref, hb_ref, pw_ref, fl_ref, fh_ref, c_ref, e_ref, q_ref, s_ref, bt_ref, x_ref
 ):
     n, _, rows, _ = y_ref.shape
     lanes = rows - 4 * ML_AZ
@@ -122,7 +122,10 @@
     def each(step, start):
         return lax.fori_loop(0, n, step, start, unroll=n <= 16)
 
-    def filtered(d, carry):
+    def groups(step, start):
+        return lax.fori_loop(0, n // 16, step, start, unroll=n <= 16)
+
+    def windows_of(d):
         windows, edges = [], []
         for part in range(2):
             v = y_ref[d, part].astype(jnp.float32).reshape(rows // 8, 8, LANES)
@@ -148,19 +151,24 @@
         if lanes < LANES:
             windows = jnp.concatenate([windows, jnp.zeros((LANES - lanes, 4 * LANES), jnp.float32)], axis=0)
         wh_ref[d] = jnp.concatenate(edges, axis=1)
-        b_ref[d] = apply_filter(m_ref[...], windows.astype(jnp.bfloat16))
-        for band in range(2):
-            pw_ref[d, band] = power_of(b_ref, d, band)
+        return windows.astype(jnp.bfloat16)
+
+    def filtered(pair, carry):
+        dates = (2 * pair, 2 * pair + 1)
+        bands = apply_filter(m_ref[...], jnp.concatenate([windows_of(d) for d in dates], axis=0))
+        for t, d in enumerate(dates):
+            b_ref[d] = bands[:, LANES * t : LANES * (t + 1)]
+            for band in range(2):
+                pw_ref[d, band] = power_of(b_ref, d, band)
         return carry
 
-    each(filtered, 0)
+    lax.fori_loop(0, n // 2, filtered, 0, unroll=n <= 16)
 
     for h in range(halos):
         hb_ref[h] = apply_filter(m_ref[...], wh_ref[16 * h : 16 * h + 16].reshape(LANES, 4 * LANES).astype(jnp.bfloat16))
 
     def pairs(d, carry):
         later = [jnp.minimum(d + k, n - 1) for k in range(1, SPAN + 1)]
-        cross, partner = [], []
         for band in range(2):
             real = [zero] * SPAN
             imag = [zero] * SPAN
@@ -172,17 +180,23 @@
                     pi = b_ref[later[k], row_of(band, 1, j)]
                     real[k] = real[k] + (r * pr + i * pi)
                     imag[k] = imag[k] + (i * pr - r * pi)
-            cross.append((group_sums(*real), group_sums(*imag)))
-            partner.append(pick4(*[pw_ref[e, band] for e in later]))
-        own = [pw_ref[d, band] for band in range(2)]
-        weight, weighted = weigh(cross, own, partner, fl_ref[d])
-        q_ref[0, d] = weight
-        q_ref[1, d] = weighted
+            c_ref[2 * band, d] = group_sums(*real)
+            c_ref[2 * band + 1, d] = group_sums(*imag)
+            c_ref[4 + band, d] = pick4(*[pw_ref[e, band] for e in later])
         return carry
 
     each(pairs, 0)
 
-    edge_sums = []
+    def weights(h, carry):
+        dates = pl.ds(16 * h, 16)
+        cross = [(c_ref[2 * band, dates], c_ref[2 * band + 1, dates]) for band in range(2)]
+        own = [pw_ref[dates, band] for band in range(2)]
+        partner = [c_ref[4 + band, dates] for band in range(2)]
+        q_ref[0, dates], q_ref[1, dates] = weigh(cross, own, partner, fl_ref[dates])
+        return carry
+
+    groups(weights, 0)
+
     hpow = [[power_of(hb_ref, h, band) for band in range(2)] for h in range(halos)]
     for h in range(halos):
         after = min(h + 1, halos - 1)
@@ -211,9 +225,9 @@
             partner.append(pick4(*[shifted(hpow[h][band], hpow[after][band], k) for k in range(1, SPAN + 1)]))
         weight, weighted = weigh(cross, hpow[h], partner, fh_ref[h])
         for which, value in enumerate((weight, weighted)):
-            upto, onward, _ = cell_sums(value)
-            wh_ref[h, :, which * 256 : which * 256 + 128] = upto
-            wh_ref[h, :, which * 256 + 128 : which * 256 + 256] = onward
+            upto, onward, _ = cell_sums(value[None])
+            e_ref[h, which, 0] = upto[0]
+            e_ref[h, which, 1] = onward[0]
 
     for d in range(SPAN):
         x_ref[0, d] = zero
@@ -221,57 +235,63 @@
         x_ref[0, n + SPAN + d] = zero
         x_ref[1, n + SPAN + d] = zero
         for k in range(SPAN):
-            s_ref[0, d, k] = zero
-            s_ref[1, d, k] = zero
-
-    def smooth(d, chain):
-        h, place = d // 16, 8 * (d % 16)
+            s_ref[0, k, d] = zero
+            s_ref[1, k, d] = zero
+
+    def smooth(h, chain):
+        dates = pl.ds(16 * h, 16)
+        wide = iota((16, 8, LANES), 2)
         boxes = []
         for which in range(2):
-            upto, onward, total = cell_sums(q_ref[which, d])
-            far_upto = pltpu.roll(wh_ref[h, :, which * 256 : which * 256 + 128], (lanes - 4 - place) % LANES, 1)
-            far_onward = pltpu.roll(wh_ref[h, :, which * 256 + 128 : which * 256 + 256], (LANES - 4 - place) % LANES, 1)
-            sooner = jnp.where(lane < 4, far_onward, pltpu.roll(onward, 4, 1))
-            later = jnp.where(lane >= lanes - 4, far_upto, back(upto, 4))
+            upto, onward, total = cell_sums(q_ref[which, dates])
+            far_upto = [pltpu.roll(e_ref[h, which, 0], (lanes - 4 - 8 * t) % LANES, 1) for t in range(16)]
+            far_onward = [pltpu.roll(e_ref[h, which, 1], (LANES - 4 - 8 * t) % LANES, 1) for t in range(16)]
+            sooner = jnp.where(wide < 4, jnp.stack(far_onward), pltpu.roll(onward, 4, 2))
+            later = jnp.where(wide >= lanes - 4, jnp.stack(far_upto), pltpu.roll(upto, LANES - 4, 2))
             boxes.append(total + sooner + later)
         phase = boxes[1] / (boxes[0] + floor_weight)
         weight = boxes[0] * (1.0 / (2 * RADIUS + 1))
         product = weight * phase
-        total_weight = zero
-        pull = ridge_weight * chain
+        own = pl.ds(16 * h + SPAN, 16)
         for k in range(SPAN):
-            s = weight if k == 0 else back(weight, k)
-            g = product if k == 0 else back(product, k)
-            s_ref[0, d + SPAN, k] = s
-            s_ref[1, d + SPAN, k] = g
-            total_weight = total_weight + s + s_ref[0, d + SPAN - 1 - k, k]
-            pull = pull - g + s_ref[1, d + SPAN - 1 - k, k]
-        x_ref[0, d + SPAN] = chain
-        bt_ref[0, d] = pull
-        bt_ref[1, d] = 1.0 / (total_weight + ridge_weight)
-        out_ref[d] = pltpu.roll(total_weight, 1, 1)
-        return chain + phase
-
-    each(smooth, zero)
+            s_ref[0, k, own] = weight if k == 0 else pltpu.roll(weight, LANES - k, 2)
+            s_ref[1, k, own] = product if k == 0 else pltpu.roll(product, LANES - k, 2)
+        for t in range(16):
+            x_ref[0, 16 * h + t + SPAN] = chain
+            chain = chain + phase[t]
+        total_weight = jnp.zeros((16, 8, LANES), jnp.float32)
+        pull = ridge_weight * x_ref[0, own]
+        for k in range(SPAN):
+            low = pl.ds(16 * h + SPAN - 1 - k, 16)
+            total_weight = total_weight + s_ref[0, k, own] + s_ref[0, k, low]
+            pull = pull - s_ref[1, k, own] + s_ref[1, k, low]
+        bt_ref[0, dates] = pull
+        bt_ref[1, dates] = 1.0 / (total_weight + ridge_weight)
+        out_ref[dates] = pltpu.roll(total_weight, 1, 2)
+        return chain
+
+    groups(smooth, zero)
 
     for sweep in range(ITERS):
         old, new = sweep % 2, (sweep + 1) % 2
 
-        def relax(d, carry):
-            total = bt_ref[0, d]
+        def relax(h, carry):
+            total = bt_ref[0, pl.ds(16 * h, 16)]
             for k in range(SPAN):
-                total = total + s_ref[0, d + SPAN, k] * x_ref[old, d + SPAN + 1 + k]
-                total = total + s_ref[0, d + SPAN - 1 - k, k] * x_ref[old, d + SPAN - 1 - k]
-            value = total * bt_ref[1, d]
-            x_ref[new, d + SPAN] = value
+                total = total + s_ref[0, k, pl.ds(16 * h + SPAN, 16)] * x_ref[old, pl.ds(16 * h + SPAN + 1 + k, 16)]
+                below = pl.ds(16 * h + SPAN - 1 - k, 16)
+                total = total + s_ref[0, k, below] * x_ref[old, below]
+            value = total * bt_ref[1, pl.ds(16 * h, 16)]
+            x_ref[new, pl.ds(16 * h + SPAN, 16)] = value
             if sweep == ITERS - 1:
-                out_ref[d] = jnp.where(lane % 4 == 1, out_ref[d], value)
+                dates = pl.ds(16 * h, 16)
+                out_ref[dates] = jnp.where(iota((16, 8, LANES), 2) % 4 == 1, out_ref[dates], value)
             return carry
 
-        each(relax, 0)
-
-
-def spread_kernel(x_ref, flags_ref, out_ref, held_ref, made_ref, in_sems, out_sems):
+        groups(relax, 0)
+
+
+def spread_kernel(x_ref, flags_ref, out_ref, held_ref, in_sems):
     parts = in_sems.shape[1]
     looks = out_ref.shape[0] // parts
     rows = out_ref.shape[2]
@@ -288,10 +308,6 @@
     def fetch(part, q):
         columns = pl.ds(q * width, width)
         return pltpu.make_async_copy(x_ref.at[0, part, :, columns], held_ref.at[part, :, columns], in_sems.at[part, q])
-
-    def send(part, q):
-        chunks = pl.ds(q * looks, looks)
-        return pltpu.make_async_copy(made_ref.at[chunks, part], out_ref.at[chunks, part], out_sems.at[part, q])
 
     for part in range(2):
         for q in range(parts):
@@ -328,11 +344,7 @@
                         if part == 0 and tile == rows // 16 - 1:
                             bottom = jnp.where((sub >= 4) & (lane >= LANES // 2), pattern, bottom)
                         both = jnp.concatenate([top, bottom], axis=0).astype(jnp.bfloat16)
-                        made_ref[q * looks + 2 * half + odd, part, 16 * tile : 16 * tile + 16, :] = both
-            send(part, q).start()
-    for part in range(2):
-        for q in range(parts):
-            send(part, q).wait()
+                        out_ref[q * looks + 2 * half + odd, part, 16 * tile : 16 * tile + 16, :] = both
 
 
 def gather_kernel(z_ref, phase_ref, weight_ref):
@@ -370,13 +382,11 @@
     params = pltpu.CompilerParams(vmem_limit_bytes=60 * 1024 * 1024)
     chunks = pl.pallas_call(
         spread_kernel,
-        out_shape=jax.ShapeDtypeStruct((n, 2, rows, LANES), jnp.bfloat16),
+        out_shape=pltpu.VMEM((n, 2, rows, LANES), jnp.bfloat16),
         in_specs=[anywhere, pl.BlockSpec(memory_space=pltpu.SMEM)],
-        out_specs=anywhere,
+        out_specs=in_vmem,
         scratch_shapes=[
             pltpu.VMEM(slc_stack.shape[1:], jnp.bfloat16),
-            pltpu.VMEM((n, 2, rows, LANES), jnp.bfloat16),
-            pltpu.SemaphoreType.DMA((2, parts)),
             pltpu.SemaphoreType.DMA((2, parts)),
         ],
         compiler_params=params,
@@ -385,14 +395,15 @@
     taps = jnp.pad(band_taps.astype(jnp.float32).reshape(4, TAPS), ((0, 0), (0, 2 * LANES - TAPS)))
     matrix = pl.pallas_call(
         filter_kernel,
-        out_shape=jax.ShapeDtypeStruct((4 * LANES, 4 * LANES), jnp.bfloat16),
+        out_shape=pltpu.VMEM((4 * LANES, 4 * LANES), jnp.bfloat16),
         in_specs=[in_vmem],
         out_specs=in_vmem,
         compiler_params=params,
     )(taps)
+    matrix = pltpu.with_memory_space_constraint(matrix, pltpu.VMEM)
     solved = pl.pallas_call(
         solve_kernel,
-        out_shape=jax.ShapeDtypeStruct((n, *tile), jnp.float32),
+        out_shape=pltpu.VMEM((n, *tile), jnp.float32),
         in_specs=[in_vmem, in_vmem],
         out_specs=in_vmem,
         scratch_shapes=[
@@ -402,8 +413,10 @@
             pltpu.VMEM((n, 2, *tile), jnp.float32),
             pltpu.VMEM((n, *tile), jnp.float32),
             pltpu.VMEM((halos, *tile), jnp.float32),
+            pltpu.VMEM((6, n, *tile), jnp.float32),
+            pltpu.VMEM((halos, 2, 2, *tile), jnp.float32),
             pltpu.VMEM((2, n, *tile), jnp.float32),
-            pltpu.VMEM((2, n + SPAN, SPAN, *tile), jnp.float32),
+            pltpu.VMEM((2, SPAN, n + SPAN, *tile), jnp.float32),
             pltpu.VMEM((2, n, *tile), jnp.float32),
             pltpu.VMEM((2, n + 2 * SPAN, *tile), jnp.float32),
         ],
@@ -419,7 +432,7 @@
                 in_specs=[in_vmem],
                 out_specs=[in_vmem] * 2,
                 compiler_params=params,
-            )(z)
+            )(pltpu.with_memory_space_constraint(z, pltpu.VMEM))
         )
     z = z[:, :, :lanes].reshape(parts, looks, CELLS, lanes // SPAN, SPAN)[..., :2]
     z = z.transpose(4, 1, 0, 3, 2).reshape(2, *shape)

time: 59.4 us -> 56.2 us (0.946)
  Pallas kernels: 13.1 us -> 9.55 us
  waiting for transfers between devices: 22.7 us -> 23.5 us
    pallas_call x3, Pallas kernels: 11.1 us -> 8.32 us  [the longest x1 4.21 us: local(): pl.pallas_call(solve_kernel, out_shape=pltpu.VMEM((n, *tile), jnp.float32...]
    all_to_all x1, waiting for transfers between devices: 22.7 us -> 23.5 us  [local(): lax.all_to_all(chunks, 'date', 0, 0, tiled=True)]
    pallas_call x1, Pallas kernels: 2.06 us -> 1.22 us  [local(): pl.pallas_call(gather_kernel, out_shape=[jax.ShapeDtypeStruct(shape, jnp....]
  transfers between devices with their start and end apart: 1 -> 1, of which waited for: 1 -> 1; matrix products, arithmetic and copies ran while one was open for 1% -> 1% of each run, Pallas kernels for 3% -> 2%
where the time goes in v3:
time: 56.2 us; the launch traced here: 55.9 us
  waiting for transfers between devices  23.5 us (42%)
  blocking collectives  14.2 us (25%)
  Pallas kernels  9.55 us (17%)
  starting transfers between devices  7.4 us (13%)
  between operations  0.68 us (1%)
  other arithmetic  0.6 us (1%)
    all_to_all x1, waiting for transfers between devices, local(): lax.all_to_all(chunks, 'date', 0, 0, tiled=True)  23.5 us
    all_to_all x1, blocking collectives, local(): z = lax.all_to_all(solved, 'date', 0, 0, tiled=True)  14.2 us
    all_to_all x1, starting transfers between devices, local(): lax.all_to_all(chunks, 'date', 0, 0, tiled=True)  7.4 us
    pallas_call x1, Pallas kernels, local(): pl.pallas_call(solve_kernel, out_shape=pltpu.VMEM((n, *tile), jnp.float32...  4.21 us
    pallas_call x1, Pallas kernels, local(): pl.pallas_call(spread_kernel, out_shape=pltpu.VMEM((n, 2, rows, LANES), j...  3.09 us
    pallas_call x1, Pallas kernels, local(): pl.pallas_call(gather_kernel, out_shape=[jax.ShapeDtypeStruct(shape, jnp....  1.22 us
  transfers between devices with their start and end apart: 1, of which 1 were waited for; matrix products, arithmetic and copies ran while one was open for 1% of the time, Pallas kernels for 2%

profile of v3, /device:TPU:0, one launch (start us, length us, event | category | flops | bytes accessed | tf_op | source)
XLA Modules:
  0.0 55.9 jit_solution(4422297892880068641)
XLA Ops:
  0.6 3.1 %shard_map.51 = bf16[16,2,144,128]{3,2,1,0:T(8,128)(2,1)} custom-call(bf16[1,2,16,16384]{3,2,1,0:T(8,128)(2,1)} %x_ref.1, s32[1,4]{1,0:T(1,128)} %flags_ref.1), custom_call_target="tpu_custom_call" | custom-call | tf_op jit(solution)/shard_map/pallas_call | solution.py:383
  3.7 0.0 copy-start
  3.7 7.4 %all-to-all-start = ((bf16[16,2,144,128]{3,2,1,0:T(8,128)(2,1)}), bf16[16,2,144,128]{3,2,1,0:T(8,128)(2,1)S(1)}, u32[]{:S(2)}, u32[]{:S(2)}) async-start(bf16[16,2,144,128]{3,2,1,0:T(8,128)(2,1)} %shard_map.51), calls=%async_computation | async-start | bytes 2359296 | tf_op jit(solution)/shard_map/all_to_all | solution.py:394
  11.1 0.0 copy-done
  11.2 0.6 %pad_convert_fusion.taps_ref = f32[4,256]{1,0:T(4,128)} fusion(bf16[4,32]{1,0:T(4,128)(2,1)S(1)} %bitcast.1), kind=kLoop, calls=%fused_computation | loop fusion | flops 1024 | bytes 4352 | tf_op jit(solution)/shard_map/jit(_pad)/pad | solution.py:395
  11.8 1.0 %shard_map.50.m_ref = bf16[512,512]{1,0:T(8,128)(2,1)S(1)} custom-call(f32[4,256]{1,0:T(4,128)} %pad_convert_fusion.taps_ref), custom_call_target="tpu_custom_call" | custom-call | tf_op jit(solution)/shard_map/pallas_call | solution.py:396
  12.8 23.5 %all-to-all-done.y_ref = bf16[16,2,144,128]{3,2,1,0:T(8,128)(2,1)S(1)} async-done(((bf16[16,2,144,128]{3,2,1,0:T(8,128)(2,1)}), bf16[16,2,144,128]{3,2,1,0:T(8,128)(2,1)S(1)}, u32[]{:S(2)}, u32[]{:S(2)}) %all-to-all-start) | async-done | bytes 1179680 | tf_op jit(solution)/shard_map/all_to_all | solution.py:394
  36.3 4.2 %shard_map.52 = f32[16,8,128]{2,1,0:T(8,128)S(1)} custom-call(bf16[512,512]{1,0:T(8,128)(2,1)S(1)} %shard_map.50.m_ref, bf16[16,2,144,128]{3,2,1,0:T(8,128)(2,1)S(1)} %all-to-all-done.y_ref), custom_call_target="tpu_custom_call" | custom-call | tf_op jit(solution)/shard_map/pallas_call | solution.py:404
  40.5 14.2 %all_to_all.10.z_ref = f32[16,8,128]{2,1,0:T(8,128)S(1)} all-to-all(f32[16,8,128]{2,1,0:T(8,128)S(1)} %shard_map.52), channel_id=1, replica_groups=mesh['group'=2,'date'=16] {'date'}, dimensions={0} | all-to-all | bytes 131072 | tf_op jit(solution)/shard_map/all_to_all | solution.py:425
  54.7 1.2 %shard_map.53 = (f32[1,4,1024]{2,1,0:T(4,128)}, f32[1,4,1024]{2,1,0:T(4,128)}) custom-call(f32[16,8,128]{2,1,0:T(8,128)S(1)} %all_to_all.10.z_ref), custom_call_target="tpu_custom_call" | custom-call | tf_op jit(solution)/shard_map/pallas_call | solution.py:429
Async XLA Ops:
  3.7 7.4 %copy-start = (bf16[2,2,32]{2,1,0:T(2,128)(2,1)S(1)}, bf16[2,2,32]{2,1,0:T(2,128)(2,1)}, u32[]{:S(2)}) copy-start(bf16[2,2,32]{2,1,0:T(2,128)(2,1)} %param.4) | copy-start | bytes 772
  3.7 32.5 %all-to-all-start = ((bf16[16,2,144,128]{3,2,1,0:T(8,128)(2,1)}), bf16[16,2,144,128]{3,2,1,0:T(8,128)(2,1)S(1)}, u32[]{:S(2)}, u32[]{:S(2)}) async-start(bf16[16,2,144,128]{3,2,1,0:T(8,128)(2,1)} %shard_map.51), calls=%async_computation | async-start | bytes 2359296 | tf_op jit(solution)/shard_map/all_to_all | solution.py:394

commit v4 on v3

--- a/solution.py
+++ b/solution.py
@@ -42,12 +42,12 @@
     return jnp.where(lane < 2, jnp.where(lane == 0, x0, x1), jnp.where(lane == 2, x2, x3))
 
 
-def filter_kernel(taps_ref, m_ref):
+def fill_filter(taps_ref, m_ref):
     width = 2 * LANES
     sub = iota((CELLS, width), 0)
 
     def placed(row):
-        taps = jnp.broadcast_to(taps_ref[row : row + 1, :], (CELLS, width))
+        taps = jnp.broadcast_to(taps_ref[row], (CELLS, width))
         result = jnp.zeros((CELLS, width), jnp.float32)
         for c in range(CELLS):
             result = jnp.where(sub == c, pltpu.roll(taps, (ML_RG * c - TAPS // 2) % width, 1), result)
@@ -291,7 +291,7 @@
         groups(relax, 0)
 
 
-def spread_kernel(x_ref, flags_ref, out_ref, held_ref, in_sems):
+def spread_kernel(x_ref, far_flags_ref, far_taps_ref, out_ref, m_ref, held_ref, flags_ref, taps_ref, wide_ref, in_sems, side_sems):
     parts = in_sems.shape[1]
     looks = out_ref.shape[0] // parts
     rows = out_ref.shape[2]
@@ -299,19 +299,30 @@
     pairs = width // (2 * LANES)
     sub = iota((8, LANES), 0)
     lane = iota((8, LANES), 1)
+    zero = jnp.zeros((8, LANES), jnp.float32)
+
+    def fetch(part, q):
+        columns = pl.ds(q * width, width)
+        return pltpu.make_async_copy(x_ref.at[0, part, :, columns], held_ref.at[part, :, columns], in_sems.at[part, q])
+
+    get_flags = pltpu.make_async_copy(far_flags_ref, flags_ref, side_sems.at[0])
+    get_taps = pltpu.make_async_copy(far_taps_ref, taps_ref, side_sems.at[1])
+    get_taps.start()
+    get_flags.start()
+    for part in range(2):
+        for q in range(parts):
+            fetch(part, q).start()
+    wide_ref[...] = jnp.zeros_like(wide_ref)
+    get_taps.wait()
+    for band in range(2):
+        for part in range(2):
+            wide_ref[2 * band + part, :, :TAPS] = taps_ref[band, part : part + 1, :].astype(jnp.float32)
+    fill_filter(wide_ref, m_ref)
+    get_flags.wait()
     flags = [flags_ref[0, k].astype(jnp.float32) for k in range(SPAN)]
     pattern = jnp.where(
         lane % 4 < 2, jnp.where(lane % 4 == 0, flags[0], flags[1]), jnp.where(lane % 4 == 2, flags[2], flags[3])
     )
-    zero = jnp.zeros((8, LANES), jnp.float32)
-
-    def fetch(part, q):
-        columns = pl.ds(q * width, width)
-        return pltpu.make_async_copy(x_ref.at[0, part, :, columns], held_ref.at[part, :, columns], in_sems.at[part, q])
-
-    for part in range(2):
-        for q in range(parts):
-            fetch(part, q).start()
     for part in range(2):
         made = {}
 
@@ -380,26 +391,25 @@
     in_vmem = pl.BlockSpec(memory_space=pltpu.VMEM)
     anywhere = pl.BlockSpec(memory_space=pl.ANY)
     params = pltpu.CompilerParams(vmem_limit_bytes=60 * 1024 * 1024)
-    chunks = pl.pallas_call(
+    chunks, matrix = pl.pallas_call(
         spread_kernel,
-        out_shape=pltpu.VMEM((n, 2, rows, LANES), jnp.bfloat16),
-        in_specs=[anywhere, pl.BlockSpec(memory_space=pltpu.SMEM)],
-        out_specs=in_vmem,
+        out_shape=[
+            pltpu.VMEM((n, 2, rows, LANES), jnp.bfloat16),
+            pltpu.VMEM((4 * LANES, 4 * LANES), jnp.bfloat16),
+        ],
+        in_specs=[anywhere] * 3,
+        out_specs=[in_vmem] * 2,
         scratch_shapes=[
             pltpu.VMEM(slc_stack.shape[1:], jnp.bfloat16),
+            pltpu.SMEM(pair_flags.shape, jnp.int32),
+            pltpu.VMEM(band_taps.shape, jnp.bfloat16),
+            pltpu.VMEM((4, 1, 2 * LANES), jnp.float32),
             pltpu.SemaphoreType.DMA((2, parts)),
+            pltpu.SemaphoreType.DMA((2,)),
         ],
         compiler_params=params,
-    )(slc_stack, pair_flags)
+    )(slc_stack, pair_flags, band_taps)
     y = pltpu.with_memory_space_constraint(lax.all_to_all(chunks, "date", 0, 0, tiled=True), pltpu.VMEM)
-    taps = jnp.pad(band_taps.astype(jnp.float32).reshape(4, TAPS), ((0, 0), (0, 2 * LANES - TAPS)))
-    matrix = pl.pallas_call(
-        filter_kernel,
-        out_shape=pltpu.VMEM((4 * LANES, 4 * LANES), jnp.bfloat16),
-        in_specs=[in_vmem],
-        out_specs=in_vmem,
-        compiler_params=params,
-    )(taps)
     matrix = pltpu.with_memory_space_constraint(matrix, pltpu.VMEM)
     solved = pl.pallas_call(
         solve_kernel,

time: 56.2 us -> 54.7 us (0.973)
  blocking collectives: 14.2 us -> 46.7 us
  waiting for transfers between devices: 23.5 us -> 0 us
  starting transfers between devices: 7.4 us -> 0 us
  Pallas kernels: 9.55 us -> 7.14 us
  other arithmetic: 0.6 us -> 0 us
    all_to_all x0 -> x1, blocking collectives: none -> 36.7 us  [local(): lax.all_to_all(chunks, 'date', 0, 0, tiled=True)]
    all_to_all x1 -> x0, waiting for transfers between devices: 23.5 us -> none  [local(): lax.all_to_all(chunks, 'date', 0, 0, tiled=True)]
    all_to_all x1 -> x0, starting transfers between devices: 7.4 us -> none  [local(): lax.all_to_all(chunks, 'date', 0, 0, tiled=True)]
    all_to_all x1, blocking collectives: 14.2 us -> 9.99 us  [local(): z = lax.all_to_all(solved, 'date', 0, 0, tiled=True)]
    pallas_call x2 -> x1, Pallas kernels: 4.11 us -> 1.7 us  [local(): pl.pallas_call(spread_kernel, out_shape=[pltpu.VMEM((n, 2, rows, LANES),...]
    pad x1 -> x0, other arithmetic: 0.6 us -> none  [local(): jnp.pad(band_taps.astype(jnp.float32).reshape(4, TAPS), ((0, 0), (0, 2 *...]
  transfers between devices with their start and end apart: 1 -> 0, of which waited for: 1 -> 0; matrix products, arithmetic and copies ran while one was open for 1% -> 0% of each run, Pallas kernels for 2% -> 0%
where the time goes in v4:
time: 54.7 us; the launch traced here: 54.4 us
  blocking collectives  46.7 us (85%)
  Pallas kernels  7.14 us (13%)
  between operations  0.65 us (1%)
    all_to_all x1, blocking collectives, local(): lax.all_to_all(chunks, 'date', 0, 0, tiled=True)  36.7 us
    all_to_all x1, blocking collectives, local(): z = lax.all_to_all(solved, 'date', 0, 0, tiled=True)  9.99 us
    pallas_call x1, Pallas kernels, local(): pl.pallas_call(solve_kernel, out_shape=pltpu.VMEM((n, *tile), jnp.float32...  4.21 us
    pallas_call x1, Pallas kernels, local(): pl.pallas_call(spread_kernel, out_shape=[pltpu.VMEM((n, 2, rows, LANES),...  1.7 us
    pallas_call x1, Pallas kernels, local(): pl.pallas_call(gather_kernel, out_shape=[jax.ShapeDtypeStruct(shape, jnp....  1.22 us

profile of v4, /device:TPU:0, one launch (start us, length us, event | category | flops | bytes accessed | tf_op | source)
XLA Modules:
  0.0 54.4 jit_solution(4994126628342499386)
XLA Ops:
  0.6 1.7 %shard_map.50 = (bf16[16,2,144,128]{3,2,1,0:T(8,128)(2,1)S(1)}, bf16[512,512]{1,0:T(8,128)(2,1)S(1)}) custom-call(bf16[1,2,16,16384]{3,2,1,0:T(8,128)(2,1)} %x_ref.1, s32[1,4]{1,0:T(1,128)} %far_flags_ref.1, bf16[2,2,32]{2,1,0:T(2,128)(2,1)} %far_taps_ref.1), custom_call_target="tpu_custom_call" | custom-call | tf_op jit(solution)/shard_map/pallas_call | solution.py:394
  2.3 36.7 %all_to_all.10.y_ref = bf16[16,2,144,128]{3,2,1,0:T(8,128)(2,1)S(1)} all-to-all(bf16[16,2,144,128]{3,2,1,0:T(8,128)(2,1)S(1)} %get-tuple-element.5), channel_id=1, replica_groups=mesh['group'=2,'date'=16] {'date'}, dimensions={0} | all-to-all | bytes 2359296 | tf_op jit(solution)/shard_map/all_to_all | solution.py:412
  39.0 4.2 %shard_map.51 = f32[16,8,128]{2,1,0:T(8,128)S(1)} custom-call(bf16[512,512]{1,0:T(8,128)(2,1)S(1)} %get-tuple-element.4.m_ref, bf16[16,2,144,128]{3,2,1,0:T(8,128)(2,1)S(1)} %all_to_all.10.y_ref), custom_call_target="tpu_custom_call" | custom-call | tf_op jit(solution)/shard_map/pallas_call | solution.py:414
  43.2 10.0 %all_to_all.11.z_ref = f32[16,8,128]{2,1,0:T(8,128)S(1)} all-to-all(f32[16,8,128]{2,1,0:T(8,128)S(1)} %shard_map.51), channel_id=1, replica_groups=mesh['group'=2,'date'=16] {'date'}, dimensions={0} | all-to-all | bytes 131072 | tf_op jit(solution)/shard_map/all_to_all | solution.py:435
  53.2 1.2 %shard_map.52 = (f32[1,4,1024]{2,1,0:T(4,128)}, f32[1,4,1024]{2,1,0:T(4,128)}) custom-call(f32[16,8,128]{2,1,0:T(8,128)S(1)} %all_to_all.11.z_ref), custom_call_target="tpu_custom_call" | custom-call | tf_op jit(solution)/shard_map/pallas_call | solution.py:439

commit v5 on v4

--- a/solution.py
+++ b/solution.py
@@ -112,8 +112,9 @@
 def solve_kernel(
     m_ref, y_ref, out_ref, b_ref, wh_ref, hb_ref, pw_ref, fl_ref, fh_ref, c_ref, e_ref, q_ref, s_ref, bt_ref, x_ref
 ):
-    n, _, rows, _ = y_ref.shape
-    lanes = rows - 4 * ML_AZ
+    n, rows, _ = y_ref.shape
+    tiles = rows // 16
+    lanes = 8 * (tiles - 1)
     halos = hb_ref.shape[0]
     lane = iota((8, LANES), 1)
     sub = iota((8, LANES), 0)
@@ -127,26 +128,29 @@
 
     def windows_of(d):
         windows, edges = [], []
+        held = y_ref[d].astype(jnp.float32).reshape(rows // 8, 8, LANES)
+        beyond = held[rows // 8 - 1]
+        main = beyond[0:1]
+        main = jnp.where(lane[:1] < LANES // 2, pltpu.roll(main, LANES // 2, 1), main)
+        fl_ref[d] = jnp.broadcast_to(main, (8, LANES))
+        side = beyond[4:5]
+        middle = (lane[:1] >= LANES // 4) & (lane[:1] < 3 * LANES // 4)
+        side = jnp.where(middle, side, pltpu.roll(side, LANES // 2, 1))
+        fh_ref[d // 16] = jnp.where(lane // 8 == d % 16, jnp.broadcast_to(side, (8, LANES)), fh_ref[d // 16])
         for part in range(2):
-            v = y_ref[d, part].astype(jnp.float32).reshape(rows // 8, 8, LANES)
-            subs = iota((rows // 8 - 1, 8, LANES), 1)
-            merged = pltpu.roll(jnp.where(subs < 4, v[1:], v[:-1]), 4, 1)
-            wide = iota((rows // 8 - 2, 8, LANES), 2)
-            edge = jnp.where(wide < LANES // 2, merged[1:], merged[:-1])
-            windows.append(v[1:-1].reshape(lanes, LANES))
+            v = held[part * tiles : (part + 1) * tiles]
+            subs = iota((tiles - 1, 8, LANES), 1)
+            wide = iota((tiles - 1, 8, LANES), 2)
+            main = pltpu.roll(jnp.where(subs < 4, v[1:], v[:-1]), 4, 1)
+            edge = jnp.where(wide < LANES // 2, v[1:], v[:-1])
+            windows.append(main.reshape(lanes, LANES))
             windows.append(edge.reshape(lanes, LANES))
-            first, second, before, final = v[0], v[1], v[rows // 8 - 2], v[rows // 8 - 1]
-            later = pltpu.roll(jnp.where(sub < 4, second, final), 4, 0)
-            sooner = pltpu.roll(jnp.where(sub < 4, first, before), 4, 0)
-            edges.append(jnp.where(sub < 4, final, first))
+            first, last = v[0], v[tiles - 1]
+            far = beyond if part == 0 else pltpu.roll(beyond, LANES - TAPS // 2, 1)
+            edges.append(pltpu.roll(jnp.where(sub < 4, first, last), 4, 0))
+            later = jnp.where(sub < 4, far, first)
+            sooner = jnp.where(sub < 4, last, far)
             edges.append(jnp.where(lane < LANES // 2, later, sooner))
-            if part == 0:
-                main = final[4:5]
-                main = jnp.where(lane[:1] < LANES // 2, pltpu.roll(main, LANES // 2, 1), main)
-                fl_ref[d] = jnp.broadcast_to(main, (8, LANES))
-                side = first[0:1]
-                side = jnp.where(lane[:1] < LANES // 2, side, pltpu.roll(side, LANES // 2, 1))
-                fh_ref[d // 16] = jnp.where(lane // 8 == d % 16, jnp.broadcast_to(side, (8, LANES)), fh_ref[d // 16])
         windows = jnp.concatenate(windows, axis=1)
         if lanes < LANES:
             windows = jnp.concatenate([windows, jnp.zeros((LANES - lanes, 4 * LANES), jnp.float32)], axis=0)
@@ -294,9 +298,10 @@
 def spread_kernel(x_ref, far_flags_ref, far_taps_ref, out_ref, m_ref, held_ref, flags_ref, taps_ref, wide_ref, in_sems, side_sems):
     parts = in_sems.shape[1]
     looks = out_ref.shape[0] // parts
-    rows = out_ref.shape[2]
     width = x_ref.shape[3] // parts
-    pairs = width // (2 * LANES)
+    blocks = width // LANES
+    pairs = blocks // 2
+    reach = TAPS // 2
     sub = iota((8, LANES), 0)
     lane = iota((8, LANES), 1)
     zero = jnp.zeros((8, LANES), jnp.float32)
@@ -309,8 +314,8 @@
     get_taps = pltpu.make_async_copy(far_taps_ref, taps_ref, side_sems.at[1])
     get_taps.start()
     get_flags.start()
-    for part in range(2):
-        for q in range(parts):
+    for q in range(parts):
+        for part in range(2):
             fetch(part, q).start()
     wide_ref[...] = jnp.zeros_like(wide_ref)
     get_taps.wait()
@@ -323,56 +328,68 @@
     pattern = jnp.where(
         lane % 4 < 2, jnp.where(lane % 4 == 0, flags[0], flags[1]), jnp.where(lane % 4 == 2, flags[2], flags[3])
     )
-    for part in range(2):
-        made = {}
-
-        def pair_of(index, half):
-            if index < 0 or index >= parts * pairs:
-                return zero, zero
-            if (index, half) not in made:
-                start = index * 2 * LANES
-                first = held_ref[part, :, start : start + LANES].astype(jnp.float32)[8 * half : 8 * half + 8]
-                second = held_ref[part, :, start + LANES : start + 2 * LANES].astype(jnp.float32)[8 * half : 8 * half + 8]
-                mixed = pltpu.roll(jnp.where(sub < 4, second, first), 4, 0)
-                made[index, half] = (jnp.where(sub < 4, first, mixed), jnp.where(sub < 4, mixed, second))
-            return made[index, half]
-
-        for q in range(parts):
+    made = {}
+
+    def half_of(part, block, half):
+        if block < 0 or block >= parts * blocks:
+            return zero
+        start = block * LANES
+        return held_ref[part, :, start : start + LANES].astype(jnp.float32)[8 * half : 8 * half + 8]
+
+    def pair_of(part, index, half):
+        if (part, index, half) not in made:
+            first = half_of(part, 2 * index - 1, half)
+            second = half_of(part, 2 * index, half)
+            mixed = pltpu.roll(jnp.where(sub < 4, second, first), 4, 0)
+            made[part, index, half] = (jnp.where(sub < 4, first, mixed), jnp.where(sub < 4, mixed, second))
+        return made[part, index, half]
+
+    def beyond(q, half, odd):
+        after, before = [], []
+        for part in range(2):
+            value = half_of(part, blocks * (q + 1) + 1, half)
+            after.append(pltpu.roll(value, 4, 0) if odd else value)
+            value = half_of(part, blocks * q - 2, half)
+            before.append(value if odd else pltpu.roll(value, 4, 0))
+        side = lane // SPAN % 2
+        inside = jnp.where(side == 0, float(q < parts - 1), float(q > 0))
+        top = jnp.where(lane < reach, after[0], jnp.where(lane < 2 * reach, pltpu.roll(after[1], reach, 1), pattern))
+        bottom = jnp.where(lane >= LANES - reach, before[0], pattern * inside)
+        bottom = jnp.where(lane < reach, pltpu.roll(before[1], reach, 1), bottom)
+        return jnp.where(sub < 4, top, bottom)
+
+    for q in range(parts):
+        for part in range(2):
             if q == 0:
                 fetch(part, 0).wait()
             if q + 1 < parts:
                 fetch(part, q + 1).wait()
-            for tile in range(rows // 16):
-                upper = q * pairs - 1 + 2 * tile
-                for half in range(looks // 2):
-                    for odd in range(2):
-                        top = pair_of(upper, half)[odd]
-                        bottom = pair_of(upper + 1, half)[odd]
-                        if part == 0 and tile == 0:
-                            side = lane // SPAN % 2
-                            inside = jnp.where(side == 0, float(q < parts - 1), float(q > 0))
-                            top = jnp.where((sub < 4) & (lane < LANES // 2), pattern * inside, top)
-                        if part == 0 and tile == rows // 16 - 1:
-                            bottom = jnp.where((sub >= 4) & (lane >= LANES // 2), pattern, bottom)
-                        both = jnp.concatenate([top, bottom], axis=0).astype(jnp.bfloat16)
-                        out_ref[q * looks + 2 * half + odd, part, 16 * tile : 16 * tile + 16, :] = both
+        for half in range(looks // 2):
+            for odd in range(2):
+                chunk = q * looks + 2 * half + odd
+                rows = [pair_of(part, q * pairs + i, half)[odd] for part in range(2) for i in range(pairs + 1)]
+                for i in range(0, len(rows), 2):
+                    both = jnp.concatenate(rows[i : i + 2], axis=0)
+                    out_ref[chunk, 8 * i : 8 * i + 16, :] = both.astype(jnp.bfloat16)
+                out_ref[chunk, 8 * len(rows) : 8 * len(rows) + 8, :] = beyond(q, half, odd).astype(jnp.bfloat16)
 
 
 def gather_kernel(z_ref, phase_ref, weight_ref):
     count = z_ref.shape[0]
     looks = phase_ref.shape[1]
     width = 2 * LANES
-    source = iota((LANES, 2 * width), 0)
-    column = iota((LANES, 2 * width), 1)
+    source = iota((3 * LANES, 2 * width), 0) % LANES
+    column = iota((3 * LANES, 2 * width), 1)
     block = column % width // CELLS
-    chosen = (source == SPAN * block + column // width).astype(jnp.float32)
-    values = z_ref[...].reshape(count * CELLS, LANES)
-    moved = jnp.dot(values, chosen, precision=lax.Precision.HIGHEST, preferred_element_type=jnp.float32)
-    row = iota((count * CELLS, 2 * width), 0)
-    column = iota((count * CELLS, 2 * width), 1)
-    moved = jnp.where(row % CELLS == column % CELLS, moved, 0.0)
-    adder = (iota((count, count * CELLS), 1) // CELLS == iota((count, count * CELLS), 0)).astype(jnp.float32)
-    lines = jnp.dot(adder, moved, precision=lax.Precision.HIGHEST, preferred_element_type=jnp.float32)
+    chosen = jnp.where(source == SPAN * block + column // width, 1.0, 0.0).astype(jnp.bfloat16)
+    rest = z_ref[...].reshape(count * CELLS, LANES)
+    pieces = []
+    for _ in range(3):
+        pieces.append(rest.astype(jnp.bfloat16))
+        rest = rest - pieces[-1].astype(jnp.float32)
+    moved = jnp.dot(jnp.concatenate(pieces, axis=1), chosen, preferred_element_type=jnp.float32)
+    moved = moved.reshape(count, CELLS, 2 * width)
+    lines = jnp.where(iota(moved.shape, 1) == iota(moved.shape, 2) % CELLS, moved, 0.0).sum(axis=1)
     for q in range(count // looks):
         for which, out in enumerate((phase_ref, weight_ref)):
             out[0, :, width * q : width * (q + 1)] = lines[
@@ -385,7 +402,7 @@
     looks = slc_stack.shape[2] // ML_AZ
     parts = n // looks
     lanes = slc_stack.shape[3] // (parts * LANES) * ML_AZ
-    rows = lanes + 4 * ML_AZ
+    rows = 2 * (lanes + 2 * ML_AZ) + 8
     halos = n * 8 // LANES
     tile = (8, LANES)
     in_vmem = pl.BlockSpec(memory_space=pltpu.VMEM)
@@ -394,7 +411,7 @@
     chunks, matrix = pl.pallas_call(
         spread_kernel,
         out_shape=[
-            pltpu.VMEM((n, 2, rows, LANES), jnp.bfloat16),
+            pltpu.VMEM((n, rows, LANES), jnp.bfloat16),
             pltpu.VMEM((4 * LANES, 4 * LANES), jnp.bfloat16),
         ],
         in_specs=[anywhere] * 3,

time: 54.7 us -> 53.7 us (0.982)
  blocking collectives: 46.7 us -> 46 us
where the time goes in v5:
time: 53.7 us; the launch traced here: 53.5 us
  blocking collectives  46 us (86%)
  Pallas kernels  6.84 us (13%)
  between operations  0.65 us (1%)
    all_to_all x1, blocking collectives, local(): lax.all_to_all(chunks, 'date', 0, 0, tiled=True)  36.3 us
    all_to_all x1, blocking collectives, local(): z = lax.all_to_all(solved, 'date', 0, 0, tiled=True)  9.77 us
    pallas_call x1, Pallas kernels, local(): pl.pallas_call(solve_kernel, out_shape=pltpu.VMEM((n, *tile), jnp.float32...  4.21 us
    pallas_call x1, Pallas kernels, local(): pl.pallas_call(spread_kernel, out_shape=[pltpu.VMEM((n, rows, LANES), jnp...  1.74 us

profile of v5, /device:TPU:0, one launch (start us, length us, event | category | flops | bytes accessed | tf_op | source)
XLA Modules:
  0.0 53.5 jit_solution(14720655746863792622)
XLA Ops:
  0.6 1.7 %shard_map.50 = (bf16[16,280,128]{2,1,0:T(8,128)(2,1)S(1)}, bf16[512,512]{1,0:T(8,128)(2,1)S(1)}) custom-call(bf16[1,2,16,16384]{3,2,1,0:T(8,128)(2,1)} %x_ref.1, s32[1,4]{1,0:T(1,128)} %far_flags_ref.1, bf16[2,2,32]{2,1,0:T(2,128)(2,1)} %far_taps_ref.1), custom_call_target="tpu_custom_call" | custom-call | tf_op jit(solution)/shard_map/pallas_call | solution.py:411
  2.4 36.3 %all_to_all.10.y_ref = bf16[16,280,128]{2,1,0:T(8,128)(2,1)S(1)} all-to-all(bf16[16,280,128]{2,1,0:T(8,128)(2,1)S(1)} %get-tuple-element.5), channel_id=1, replica_groups=mesh['group'=2,'date'=16] {'date'}, dimensions={0} | all-to-all | bytes 2293760 | tf_op jit(solution)/shard_map/all_to_all | solution.py:429
  38.6 4.2 %shard_map.51 = f32[16,8,128]{2,1,0:T(8,128)S(1)} custom-call(bf16[512,512]{1,0:T(8,128)(2,1)S(1)} %get-tuple-element.4.m_ref, bf16[16,280,128]{2,1,0:T(8,128)(2,1)S(1)} %all_to_all.10.y_ref), custom_call_target="tpu_custom_call" | custom-call | tf_op jit(solution)/shard_map/pallas_call | solution.py:431
  42.9 9.8 %all_to_all.11.z_ref = f32[16,8,128]{2,1,0:T(8,128)S(1)} all-to-all(f32[16,8,128]{2,1,0:T(8,128)S(1)} %shard_map.51), channel_id=1, replica_groups=mesh['group'=2,'date'=16] {'date'}, dimensions={0} | all-to-all | bytes 131072 | tf_op jit(solution)/shard_map/all_to_all | solution.py:452
  52.6 0.9 %shard_map.52 = (f32[1,4,1024]{2,1,0:T(4,128)}, f32[1,4,1024]{2,1,0:T(4,128)}) custom-call(f32[16,8,128]{2,1,0:T(8,128)S(1)} %all_to_all.11.z_ref), custom_call_target="tpu_custom_call" | custom-call | tf_op jit(solution)/shard_map/pallas_call | solution.py:456

commit v6 on v5

--- a/solution.py
+++ b/solution.py
@@ -110,12 +110,13 @@
 
 
 def solve_kernel(
-    m_ref, y_ref, out_ref, b_ref, wh_ref, hb_ref, pw_ref, fl_ref, fh_ref, c_ref, e_ref, q_ref, s_ref, bt_ref, x_ref
+    m_ref, y_ref, out_ref, b_ref, u_ref, wh_ref, hb_ref, pw_ref, fl_ref, fh_ref, c_ref, e_ref, q_ref, s_ref, bt_ref, x_ref
 ):
     n, rows, _ = y_ref.shape
     tiles = rows // 16
     lanes = 8 * (tiles - 1)
     halos = hb_ref.shape[0]
+    kept = u_ref.shape[0] == n
     lane = iota((8, LANES), 1)
     sub = iota((8, LANES), 0)
     zero = jnp.zeros((8, LANES), jnp.float32)
@@ -161,7 +162,13 @@
         dates = (2 * pair, 2 * pair + 1)
         bands = apply_filter(m_ref[...], jnp.concatenate([windows_of(d) for d in dates], axis=0))
         for t, d in enumerate(dates):
-            b_ref[d] = bands[:, LANES * t : LANES * (t + 1)]
+            own = bands[:, LANES * t : LANES * (t + 1)]
+            b_ref[d] = own
+            for band in range(2 if kept else 0):
+                real = own[2 * band * LANES : (2 * band + 1) * LANES]
+                imag = own[(2 * band + 1) * LANES : (2 * band + 2) * LANES]
+                u_ref[d, 2 * band * LANES : (2 * band + 1) * LANES] = real + imag
+                u_ref[d, (2 * band + 1) * LANES : (2 * band + 2) * LANES] = real - imag
             for band in range(2):
                 pw_ref[d, band] = power_of(b_ref, d, band)
         return carry
@@ -171,21 +178,28 @@
     for h in range(halos):
         hb_ref[h] = apply_filter(m_ref[...], wh_ref[16 * h : 16 * h + 16].reshape(LANES, 4 * LANES).astype(jnp.bfloat16))
 
+    def mixed(d, band, j, which):
+        if kept:
+            return u_ref[d, row_of(band, which, j)]
+        real, imag = b_ref[d, row_of(band, 0, j)], b_ref[d, row_of(band, 1, j)]
+        return real - imag if which else real + imag
+
     def pairs(d, carry):
         later = [jnp.minimum(d + k, n - 1) for k in range(1, SPAN + 1)]
         for band in range(2):
-            real = [zero] * SPAN
-            imag = [zero] * SPAN
+            shared = [zero] * SPAN
+            plus = [zero] * SPAN
+            minus = [zero] * SPAN
             for j in range(ML_RG):
                 r = b_ref[d, row_of(band, 0, j)]
                 i = b_ref[d, row_of(band, 1, j)]
+                both = mixed(d, band, j, 0)
                 for k in range(SPAN):
-                    pr = b_ref[later[k], row_of(band, 0, j)]
-                    pi = b_ref[later[k], row_of(band, 1, j)]
-                    real[k] = real[k] + (r * pr + i * pi)
-                    imag[k] = imag[k] + (i * pr - r * pi)
-            c_ref[2 * band, d] = group_sums(*real)
-            c_ref[2 * band + 1, d] = group_sums(*imag)
+                    shared[k] = shared[k] + both * b_ref[later[k], row_of(band, 0, j)]
+                    plus[k] = plus[k] + r * mixed(later[k], band, j, 0)
+                    minus[k] = minus[k] + i * mixed(later[k], band, j, 1)
+            c_ref[2 * band, d] = group_sums(*[a - b for a, b in zip(shared, minus)])
+            c_ref[2 * band + 1, d] = group_sums(*[a - b for a, b in zip(shared, plus)])
             c_ref[4 + band, d] = pick4(*[pw_ref[e, band] for e in later])
         return carry
 
@@ -435,6 +449,7 @@
         out_specs=in_vmem,
         scratch_shapes=[
             pltpu.VMEM((n, 4 * LANES, LANES), jnp.float32),
+            pltpu.VMEM((n if n <= 32 else 1, 4 * LANES, LANES), jnp.float32),
             pltpu.VMEM((n, 8, 4 * LANES), jnp.float32),
             pltpu.VMEM((halos, 4 * LANES, LANES), jnp.float32),
             pltpu.VMEM((n, 2, *tile), jnp.float32),

time: 53.7 us -> 53.5 us (level)
  no operation moved by 1% of the time
where the time goes in v6:
time: 53.5 us; the launch traced here: 53.3 us
  blocking collectives  46 us (86%)
  Pallas kernels  6.57 us (12%)
  between operations  0.65 us (1%)
    all_to_all x1, blocking collectives, local(): lax.all_to_all(chunks, 'date', 0, 0, tiled=True)  36.3 us
    all_to_all x1, blocking collectives, local(): z = lax.all_to_all(solved, 'date', 0, 0, tiled=True)  9.78 us
    pallas_call x1, Pallas kernels, local(): pl.pallas_call(solve_kernel, out_shape=pltpu.VMEM((n, *tile), jnp.float32...  3.94 us
    pallas_call x1, Pallas kernels, local(): pl.pallas_call(spread_kernel, out_shape=[pltpu.VMEM((n, rows, LANES), jnp...  1.74 us

profile of v6, /device:TPU:0, one launch (start us, length us, event | category | flops | bytes accessed | tf_op | source)
XLA Modules:
  0.0 53.3 jit_solution(2283065578257636029)
XLA Ops:
  0.6 1.7 %shard_map.50 = (bf16[16,280,128]{2,1,0:T(8,128)(2,1)S(1)}, bf16[512,512]{1,0:T(8,128)(2,1)S(1)}) custom-call(bf16[1,2,16,16384]{3,2,1,0:T(8,128)(2,1)} %x_ref.1, s32[1,4]{1,0:T(1,128)} %far_flags_ref.1, bf16[2,2,32]{2,1,0:T(2,128)(2,1)} %far_taps_ref.1), custom_call_target="tpu_custom_call" | custom-call | tf_op jit(solution)/shard_map/pallas_call | solution.py:425
  2.4 36.3 %all_to_all.10.y_ref = bf16[16,280,128]{2,1,0:T(8,128)(2,1)S(1)} all-to-all(bf16[16,280,128]{2,1,0:T(8,128)(2,1)S(1)} %get-tuple-element.5), channel_id=1, replica_groups=mesh['group'=2,'date'=16] {'date'}, dimensions={0} | all-to-all | bytes 2293760 | tf_op jit(solution)/shard_map/all_to_all | solution.py:443
  38.6 3.9 %shard_map.51 = f32[16,8,128]{2,1,0:T(8,128)S(1)} custom-call(bf16[512,512]{1,0:T(8,128)(2,1)S(1)} %get-tuple-element.4.m_ref, bf16[16,280,128]{2,1,0:T(8,128)(2,1)S(1)} %all_to_all.10.y_ref), custom_call_target="tpu_custom_call" | custom-call | tf_op jit(solution)/shard_map/pallas_call | solution.py:445
  42.6 9.8 %all_to_all.11.z_ref = f32[16,8,128]{2,1,0:T(8,128)S(1)} all-to-all(f32[16,8,128]{2,1,0:T(8,128)S(1)} %shard_map.51), channel_id=1, replica_groups=mesh['group'=2,'date'=16] {'date'}, dimensions={0} | all-to-all | bytes 131072 | tf_op jit(solution)/shard_map/all_to_all | solution.py:467
  52.4 0.9 %shard_map.52 = (f32[1,4,1024]{2,1,0:T(4,128)}, f32[1,4,1024]{2,1,0:T(4,128)}) custom-call(f32[16,8,128]{2,1,0:T(8,128)S(1)} %all_to_all.11.z_ref), custom_call_target="tpu_custom_call" | custom-call | tf_op jit(solution)/shard_map/pallas_call | solution.py:471

commit v7 on v6

--- a/solution.py
+++ b/solution.py
@@ -120,9 +120,6 @@
     lane = iota((8, LANES), 1)
     sub = iota((8, LANES), 0)
     zero = jnp.zeros((8, LANES), jnp.float32)
-
-    def each(step, start):
-        return lax.fori_loop(0, n, step, start, unroll=n <= 16)
 
     def groups(step, start):
         return lax.fori_loop(0, n // 16, step, start, unroll=n <= 16)
@@ -173,11 +170,6 @@
                 pw_ref[d, band] = power_of(b_ref, d, band)
         return carry
 
-    lax.fori_loop(0, n // 2, filtered, 0, unroll=n <= 16)
-
-    for h in range(halos):
-        hb_ref[h] = apply_filter(m_ref[...], wh_ref[16 * h : 16 * h + 16].reshape(LANES, 4 * LANES).astype(jnp.bfloat16))
-
     def mixed(d, band, j, which):
         if kept:
             return u_ref[d, row_of(band, which, j)]
@@ -185,7 +177,7 @@
         return real - imag if which else real + imag
 
     def pairs(d, carry):
-        later = [jnp.minimum(d + k, n - 1) for k in range(1, SPAN + 1)]
+        later = [min(d + k, n - 1) if n <= 16 else jnp.minimum(d + k, n - 1) for k in range(1, SPAN + 1)]
         for band in range(2):
             shared = [zero] * SPAN
             plus = [zero] * SPAN
@@ -203,7 +195,18 @@
             c_ref[4 + band, d] = pick4(*[pw_ref[e, band] for e in later])
         return carry
 
-    each(pairs, 0)
+    if n <= 16:
+        for d in range(0, n + SPAN, 2):
+            if d < n:
+                filtered(d // 2, 0)
+            for due in range(max(0, d - SPAN), d - SPAN + 2):
+                pairs(due, 0)
+    else:
+        lax.fori_loop(0, n // 2, filtered, 0)
+        lax.fori_loop(0, n, pairs, 0)
+
+    for h in range(halos):
+        hb_ref[h] = apply_filter(m_ref[...], wh_ref[16 * h : 16 * h + 16].reshape(LANES, 4 * LANES).astype(jnp.bfloat16))
 
     def weights(h, carry):
         dates = pl.ds(16 * h, 16)

time: 53.5 us -> 53.5 us (level)
  no operation moved by 1% of the time
where the time goes in v7:
time: 53.5 us; the launch traced here: 53.3 us
  blocking collectives  46 us (86%)
  Pallas kernels  6.57 us (12%)
  between operations  0.65 us (1%)
    all_to_all x1, blocking collectives, local(): lax.all_to_all(chunks, 'date', 0, 0, tiled=True)  36.3 us
    all_to_all x1, blocking collectives, local(): z = lax.all_to_all(solved, 'date', 0, 0, tiled=True)  9.78 us
    pallas_call x1, Pallas kernels, local(): pl.pallas_call(solve_kernel, out_shape=pltpu.VMEM((n, *tile), jnp.float32...  3.94 us
    pallas_call x1, Pallas kernels, local(): pl.pallas_call(spread_kernel, out_shape=[pltpu.VMEM((n, rows, LANES), jnp...  1.74 us

profile of v7, /device:TPU:0, one launch (start us, length us, event | category | flops | bytes accessed | tf_op | source)
XLA Modules:
  0.0 53.3 jit_solution(1365467421092063872)
XLA Ops:
  0.6 1.7 %shard_map.50 = (bf16[16,280,128]{2,1,0:T(8,128)(2,1)S(1)}, bf16[512,512]{1,0:T(8,128)(2,1)S(1)}) custom-call(bf16[1,2,16,16384]{3,2,1,0:T(8,128)(2,1)} %x_ref.1, s32[1,4]{1,0:T(1,128)} %far_flags_ref.1, bf16[2,2,32]{2,1,0:T(2,128)(2,1)} %far_taps_ref.1), custom_call_target="tpu_custom_call" | custom-call | tf_op jit(solution)/shard_map/pallas_call | solution.py:428
  2.4 36.3 %all_to_all.10.y_ref = bf16[16,280,128]{2,1,0:T(8,128)(2,1)S(1)} all-to-all(bf16[16,280,128]{2,1,0:T(8,128)(2,1)S(1)} %get-tuple-element.5), channel_id=1, replica_groups=mesh['group'=2,'date'=16] {'date'}, dimensions={0} | all-to-all | bytes 2293760 | tf_op jit(solution)/shard_map/all_to_all | solution.py:446
  38.6 3.9 %shard_map.51 = f32[16,8,128]{2,1,0:T(8,128)S(1)} custom-call(bf16[512,512]{1,0:T(8,128)(2,1)S(1)} %get-tuple-element.4.m_ref, bf16[16,280,128]{2,1,0:T(8,128)(2,1)S(1)} %all_to_all.10.y_ref), custom_call_target="tpu_custom_call" | custom-call | tf_op jit(solution)/shard_map/pallas_call | solution.py:448
  42.6 9.8 %all_to_all.11.z_ref = f32[16,8,128]{2,1,0:T(8,128)S(1)} all-to-all(f32[16,8,128]{2,1,0:T(8,128)S(1)} %shard_map.51), channel_id=1, replica_groups=mesh['group'=2,'date'=16] {'date'}, dimensions={0} | all-to-all | bytes 131072 | tf_op jit(solution)/shard_map/all_to_all | solution.py:470
  52.4 0.9 %shard_map.52 = (f32[1,4,1024]{2,1,0:T(4,128)}, f32[1,4,1024]{2,1,0:T(4,128)}) custom-call(f32[16,8,128]{2,1,0:T(8,128)S(1)} %all_to_all.11.z_ref), custom_call_target="tpu_custom_call" | custom-call | tf_op jit(solution)/shard_map/pallas_call | solution.py:474

commit v8 on v6

--- a/solution.py
+++ b/solution.py
@@ -169,7 +169,9 @@
                 imag = own[(2 * band + 1) * LANES : (2 * band + 2) * LANES]
                 u_ref[d, 2 * band * LANES : (2 * band + 1) * LANES] = real + imag
                 u_ref[d, (2 * band + 1) * LANES : (2 * band + 2) * LANES] = real - imag
-            for band in range(2):
+                squares = (real * real + imag * imag).reshape(ML_RG, CELLS, LANES).sum(axis=0)
+                pw_ref[d, band] = group_sums(squares, squares, squares, squares)
+            for band in range(0 if kept else 2):
                 pw_ref[d, band] = power_of(b_ref, d, band)
         return carry
 

time: 53.5 us -> 53.5 us (level)
  no operation moved by 1% of the time
where the time goes in v8:
time: 53.5 us; the launch traced here: 53.3 us
  blocking collectives  46.1 us (86%)
  Pallas kernels  6.59 us (12%)
  between operations  0.65 us (1%)
    all_to_all x1, blocking collectives, local(): lax.all_to_all(chunks, 'date', 0, 0, tiled=True)  36.3 us
    all_to_all x1, blocking collectives, local(): z = lax.all_to_all(solved, 'date', 0, 0, tiled=True)  9.79 us
    pallas_call x1, Pallas kernels, local(): pl.pallas_call(solve_kernel, out_shape=pltpu.VMEM((n, *tile), jnp.float32...  3.96 us
    pallas_call x1, Pallas kernels, local(): pl.pallas_call(spread_kernel, out_shape=[pltpu.VMEM((n, rows, LANES), jnp...  1.74 us

profile of v8, /device:TPU:0, one launch (start us, length us, event | category | flops | bytes accessed | tf_op | source)
XLA Modules:
  0.0 53.3 jit_solution(12188801540694568407)
XLA Ops:
  0.6 1.7 %shard_map.50 = (bf16[16,280,128]{2,1,0:T(8,128)(2,1)S(1)}, bf16[512,512]{1,0:T(8,128)(2,1)S(1)}) custom-call(bf16[1,2,16,16384]{3,2,1,0:T(8,128)(2,1)} %x_ref.1, s32[1,4]{1,0:T(1,128)} %far_flags_ref.1, bf16[2,2,32]{2,1,0:T(2,128)(2,1)} %far_taps_ref.1), custom_call_target="tpu_custom_call" | custom-call | tf_op jit(solution)/shard_map/pallas_call | solution.py:427
  2.4 36.3 %all_to_all.10.y_ref = bf16[16,280,128]{2,1,0:T(8,128)(2,1)S(1)} all-to-all(bf16[16,280,128]{2,1,0:T(8,128)(2,1)S(1)} %get-tuple-element.5), channel_id=1, replica_groups=mesh['group'=2,'date'=16] {'date'}, dimensions={0} | all-to-all | bytes 2293760 | tf_op jit(solution)/shard_map/all_to_all | solution.py:445
  38.6 4.0 %shard_map.51 = f32[16,8,128]{2,1,0:T(8,128)S(1)} custom-call(bf16[512,512]{1,0:T(8,128)(2,1)S(1)} %get-tuple-element.4.m_ref, bf16[16,280,128]{2,1,0:T(8,128)(2,1)S(1)} %all_to_all.10.y_ref), custom_call_target="tpu_custom_call" | custom-call | tf_op jit(solution)/shard_map/pallas_call | solution.py:447
  42.6 9.8 %all_to_all.11.z_ref = f32[16,8,128]{2,1,0:T(8,128)S(1)} all-to-all(f32[16,8,128]{2,1,0:T(8,128)S(1)} %shard_map.51), channel_id=1, replica_groups=mesh['group'=2,'date'=16] {'date'}, dimensions={0} | all-to-all | bytes 131072 | tf_op jit(solution)/shard_map/all_to_all | solution.py:469
  52.4 0.9 %shard_map.52 = (f32[1,4,1024]{2,1,0:T(4,128)}, f32[1,4,1024]{2,1,0:T(4,128)}) custom-call(f32[16,8,128]{2,1,0:T(8,128)S(1)} %all_to_all.11.z_ref), custom_call_target="tpu_custom_call" | custom-call | tf_op jit(solution)/shard_map/pallas_call | solution.py:473

commit v9 on v6

--- a/solution.py
+++ b/solution.py
@@ -159,7 +159,7 @@
         return windows.astype(jnp.bfloat16)
 
     def filtered(pair, carry):
-        dates = (2 * pair, 2 * pair + 1)
+        dates = [4 * pair + t for t in range(4)]
         bands = apply_filter(m_ref[...], jnp.concatenate([windows_of(d) for d in dates], axis=0))
         for t, d in enumerate(dates):
             own = bands[:, LANES * t : LANES * (t + 1)]
@@ -173,7 +173,7 @@
                 pw_ref[d, band] = power_of(b_ref, d, band)
         return carry
 
-    lax.fori_loop(0, n // 2, filtered, 0, unroll=n <= 16)
+    lax.fori_loop(0, n // 4, filtered, 0, unroll=n <= 16)
 
     for h in range(halos):
         hb_ref[h] = apply_filter(m_ref[...], wh_ref[16 * h : 16 * h + 16].reshape(LANES, 4 * LANES).astype(jnp.bfloat16))

time: 53.5 us -> 53.4 us (level)
  no operation moved by 1% of the time
where the time goes in v9:
time: 53.4 us; the launch traced here: 53.2 us
  blocking collectives  46 us (86%)
  Pallas kernels  6.52 us (12%)
  between operations  0.65 us (1%)
    all_to_all x1, blocking collectives, local(): lax.all_to_all(chunks, 'date', 0, 0, tiled=True)  36.3 us
    all_to_all x1, blocking collectives, local(): z = lax.all_to_all(solved, 'date', 0, 0, tiled=True)  9.77 us
    pallas_call x1, Pallas kernels, local(): pl.pallas_call(solve_kernel, out_shape=pltpu.VMEM((n, *tile), jnp.float32...  3.89 us
    pallas_call x1, Pallas kernels, local(): pl.pallas_call(spread_kernel, out_shape=[pltpu.VMEM((n, rows, LANES), jnp...  1.74 us

profile of v9, /device:TPU:0, one launch (start us, length us, event | category | flops | bytes accessed | tf_op | source)
XLA Modules:
  0.0 53.2 jit_solution(250193147961752960)
XLA Ops:
  0.6 1.7 %shard_map.50 = (bf16[16,280,128]{2,1,0:T(8,128)(2,1)S(1)}, bf16[512,512]{1,0:T(8,128)(2,1)S(1)}) custom-call(bf16[1,2,16,16384]{3,2,1,0:T(8,128)(2,1)} %x_ref.1, s32[1,4]{1,0:T(1,128)} %far_flags_ref.1, bf16[2,2,32]{2,1,0:T(2,128)(2,1)} %far_taps_ref.1), custom_call_target="tpu_custom_call" | custom-call | tf_op jit(solution)/shard_map/pallas_call | solution.py:425
  2.4 36.3 %all_to_all.10.y_ref = bf16[16,280,128]{2,1,0:T(8,128)(2,1)S(1)} all-to-all(bf16[16,280,128]{2,1,0:T(8,128)(2,1)S(1)} %get-tuple-element.5), channel_id=1, replica_groups=mesh['group'=2,'date'=16] {'date'}, dimensions={0} | all-to-all | bytes 2293760 | tf_op jit(solution)/shard_map/all_to_all | solution.py:443
  38.6 3.9 %shard_map.51 = f32[16,8,128]{2,1,0:T(8,128)S(1)} custom-call(bf16[512,512]{1,0:T(8,128)(2,1)S(1)} %get-tuple-element.4.m_ref, bf16[16,280,128]{2,1,0:T(8,128)(2,1)S(1)} %all_to_all.10.y_ref), custom_call_target="tpu_custom_call" | custom-call | tf_op jit(solution)/shard_map/pallas_call | solution.py:445
  42.5 9.8 %all_to_all.11.z_ref = f32[16,8,128]{2,1,0:T(8,128)S(1)} all-to-all(f32[16,8,128]{2,1,0:T(8,128)S(1)} %shard_map.51), channel_id=1, replica_groups=mesh['group'=2,'date'=16] {'date'}, dimensions={0} | all-to-all | bytes 131072 | tf_op jit(solution)/shard_map/all_to_all | solution.py:467
  52.3 0.9 %shard_map.52 = (f32[1,4,1024]{2,1,0:T(4,128)}, f32[1,4,1024]{2,1,0:T(4,128)}) custom-call(f32[16,8,128]{2,1,0:T(8,128)S(1)} %all_to_all.11.z_ref), custom_call_target="tpu_custom_call" | custom-call | tf_op jit(solution)/shard_map/pallas_call | solution.py:471
